TPU v7x, 32 devices: a whole 2x2x4 slice. The times are simulated.
32 devices in a mesh: groups: 2 (over x), expert: 4 (over y, core), dp: 4 (over z).
Axes of the slice: x: 2, y: 2, z: 4, core: 2. Of those that a mesh axis runs over, the one named last changes fastest.
Arguments:
- tokens: bfloat16 [4096, 7168], P(('groups', 'expert', 'dp')), parts along dimension 0, may hold values from -6 to 6
- cotangent: bfloat16 [4096, 7168], P(('groups', 'expert', 'dp')), parts along dimension 0, may hold values from -1.1953125 to 1.1953125
- route_ids: int32 [4096, 8], P(('groups', 'expert', 'dp')), parts along dimension 0, may hold values from 0 to 255, as said below
- route_weight: bfloat16 [4096, 8], P(('groups', 'expert', 'dp')), parts along dimension 0, may hold values from 0.049804688 to 0.5
- gate_weight: bfloat16 [4, 7168, 1024], P('expert', None, 'dp'), may hold values from -0.0625 to 0.0625
- up_weight: bfloat16 [4, 7168, 1024], P('expert', None, 'dp'), may hold values from -0.0625 to 0.0625
- down_weight: bfloat16 [4, 1024, 7168], P('expert', 'dp'), may hold values from -0.0625 to 0.0625
Outputs:
- grad_gate: bfloat16 [8, 7168, 1024], P(('groups', 'expert'), None, 'dp'), parts along dimension 0
- grad_up: bfloat16 [8, 7168, 1024], P(('groups', 'expert'), None, 'dp'), parts along dimension 0
- route_grad: float32 [4096, 8], P(('groups', 'expert', 'dp')), parts along dimension 0
There are 2 independent parts, one for each index of `groups`. A program takes and returns all parts, laid end to end along the dimension named above; an argument that names none is the same for every part. Nothing has to cross between parts.
Inputs may be any that keep to these rules, and one draw needn't show every extreme that they name: `route_ids`: each token names 8 different experts. Of the tokens of one device (aligned blocks of 128 rows), at most 8 name any one expert below 4, and one such expert is named by exactly 8 tokens of every device.
All inputs are finite; a program needn't handle non-finite values.
Results may differ from a plain program's by a relative error of at most 0.0049.
Values may be sent and summed in bfloat16 or wider, within the bound.
A program may use at most 128 MiB of HBM per device.

v0:
```python
import jax
import jax.numpy as jnp
from jax import lax
from jax.sharding import PartitionSpec as P

CAP = 8


def local(tokens, cotangent, route_ids, route_weight, gate_weight, up_weight, down_weight):
    expert_count = lax.axis_size("expert")
    dp_count = lax.axis_size("dp")
    tok_count, model_width = tokens.shape
    route_count = route_ids.shape[1]
    slot_count = tok_count * route_count
    flat_ids = route_ids.reshape(slot_count)
    onehot = (flat_ids[:, None] == jnp.arange(expert_count, dtype=jnp.int32)[None, :]).astype(
        jnp.int32
    )
    before = jnp.cumsum(onehot, axis=0) - onehot
    slot_rank = jnp.sum(before * onehot, axis=1)
    is_valid = flat_ids < expert_count
    target = jnp.where(is_valid, flat_ids * CAP + slot_rank, expert_count * CAP)
    slot_index = jnp.arange(slot_count, dtype=jnp.int32)
    token_table = (
        jnp.full((expert_count * CAP,), tok_count, jnp.int32)
        .at[target]
        .set(slot_index // route_count, mode="drop")
    )
    slot_table = (
        jnp.full((expert_count * CAP,), slot_count, jnp.int32)
        .at[target]
        .set(slot_index, mode="drop")
    )
    weight_table = (
        jnp.zeros((expert_count * CAP,), jnp.bfloat16)
        .at[target]
        .set(route_weight.reshape(slot_count), mode="drop")
    )
    blank_row = jnp.zeros((1, model_width), jnp.bfloat16)
    send_rows = jnp.concatenate([tokens, blank_row], axis=0)[token_table].reshape(
        expert_count, CAP, model_width
    )
    send_cots = jnp.concatenate([cotangent, blank_row], axis=0)[token_table].reshape(
        expert_count, CAP, model_width
    )
    send_weight = weight_table.reshape(expert_count, CAP)
    w_gate = gate_weight[0]
    w_up = up_weight[0]
    w_down = down_weight[0]

    def widen_rows(array):
        spread = jnp.broadcast_to(array[:, None], (expert_count, dp_count) + array.shape[1:])
        return spread.reshape((expert_count * dp_count,) + array.shape[1:])

    arrived = (
        lax.all_to_all(
            widen_rows(send_rows), ("expert", "dp"), split_axis=0, concat_axis=0, tiled=True
        ),
        lax.all_to_all(
            widen_rows(send_cots), ("expert", "dp"), split_axis=0, concat_axis=0, tiled=True
        ),
        lax.all_to_all(
            widen_rows(send_weight), ("expert", "dp"), split_axis=0, concat_axis=0, tiled=True
        ),
    )
    row_block = arrived[0].reshape(-1, model_width)
    cot_block = arrived[1].reshape(-1, model_width)
    weights = arrived[2].reshape(-1).astype(jnp.float32)
    gate_pre = jnp.dot(row_block, w_gate, preferred_element_type=jnp.float32)
    up_pre = jnp.dot(row_block, w_up, preferred_element_type=jnp.float32)
    back_proj = lax.dot_general(
        cot_block, w_down, (((1,), (1,)), ((), ())), preferred_element_type=jnp.float32
    )
    gate_sig = jax.nn.sigmoid(gate_pre)
    gate_act = gate_pre * gate_sig
    summed = jnp.sum(gate_act * up_pre * back_proj, axis=1).reshape(arrived[2].shape)
    partial_value = summed
    act_grad = weights[:, None] * back_proj
    d_gate = (act_grad * up_pre * gate_sig * (1.0 + gate_pre * (1.0 - gate_sig))).astype(
        jnp.bfloat16
    )
    d_up = (act_grad * gate_act).astype(jnp.bfloat16)
    grad_g = lax.dot_general(
        row_block, d_gate, (((0,), (0,)), ((), ())), preferred_element_type=jnp.float32
    )
    grad_u = lax.dot_general(
        row_block, d_up, (((0,), (0,)), ((), ())), preferred_element_type=jnp.float32
    )
    grad_g, grad_u, partial_value = (grad_g, grad_u, partial_value)
    returned = lax.all_to_all(
        partial_value, ("expert", "dp"), split_axis=0, concat_axis=0, tiled=True
    )
    slot_sums = jnp.sum(returned.reshape(expert_count, dp_count, CAP), axis=1)
    route_grad = (
        jnp.zeros((slot_count,), jnp.float32).at[slot_table].set(slot_sums.reshape(-1), mode="drop")
    )
    return (
        grad_g.astype(jnp.bfloat16)[None],
        grad_u.astype(jnp.bfloat16)[None],
        route_grad.reshape(tok_count, route_count),
    )


def solution(mesh):
    return jax.shard_map(
        local,
        mesh=mesh,
        in_specs=(
            P(("groups", "expert", "dp"), None),
            P(("groups", "expert", "dp"), None),
            P(("groups", "expert", "dp"), None),
            P(("groups", "expert", "dp"), None),
            P("expert", None, "dp"),
            P("expert", None, "dp"),
            P("expert", "dp", None),
        ),
        out_specs=(
            P(("groups", "expert"), None, "dp"),
            P(("groups", "expert"), None, "dp"),
            P(("groups", "expert", "dp"), None),
        ),
        check_vma=False,
    )
```

profile of v0, /device:TPU:0, one launch (start us, length us, event | category | flops | bytes accessed | tf_op | source)
XLA Modules:
  0.0 145.6 jit_solution(12111803018519198005)
XLA Ops:
  0.6 0.7 broadcast_compare_fusion
  1.3 0.7 broadcast_multiply_fusion
  2.0 0.8 copy.18
  2.8 0.1 eq.29
  2.9 0.1 eq.25
  3.0 0.1 copy.16
  3.1 0.1 lt.37
  3.2 0.8 copy.20
  4.0 0.1 reshape.149
  4.1 0.1 copy.17
  4.2 0.1 mul.53
  4.3 1.1 reduce-window.6
  5.5 0.2 slice_reduce_fusion
  5.7 0.2 reduce-window.9
  5.9 0.1 add_bitcast_fusion
  6.0 7.6 %scatter_custom_fusion.1 = bf16[32]{0:T(256)(128)(2,1)S(1)} fusion(s32[1024]{0:T(1024)S(1)} %bitcast.69, bf16[1024]{0:T(1024)(128)(2,1)S(1)} %reshape.149, bf16[]{:T(256)} %constant.14.clone.1), kind=kCustom, calls=%fused_computation.56 | custom fusion | bytes 66 | tf_op jit(solution)/shard_map/scatter | solution.py:37
  13.6 0.1 broadcast_in_dim.59
  13.7 0.6 copy.21
  14.3 7.4 %all-to-all-start.1 = ((bf16[16,1,8]{2,1,0:T(2,128)(2,1)}), bf16[16,1,8]{2,1,0:T(2,128)(2,1)S(1)}, u32[]{:S(2)}, u32[]{:S(2)}) async-start(bf16[16,1,8]{2,1,0:T(2,128)(2,1)} %copy.21), calls=%async_computation.1 | async-start | bytes 16384 | tf_op jit(solution)/shard_map/all_to_all | solution.py:62
  21.7 4.3 %scatter_custom_fusion = s32[32]{0:T(128)S(1)} fusion(s32[1024]{0:T(1024)S(1)} %bitcast.70, s32[1024]{0:T(1024)S(1)} %add_select_fusion, s32[]{:T(128)} %constant.15.clone.1), kind=kCustom, calls=%fused_computation.58 | custom fusion | bytes 132 | tf_op jit(solution)/shard_map/scatter | solution.py:27
  26.0 1.7 %concatenate.6 = bf16[129,7168]{1,0:T(8,128)(2,1)S(1)} pad(bf16[128,7168]{1,0:T(8,128)(2,1)} %param.7, bf16[]{:T(256)} %constant.14.clone.1), padding=0_1x0_0 | pad | bytes 3684354 | tf_op jit(solution)/shard_map/concatenate | solution.py:40
  27.7 0.8 gather_fusion
  28.6 0.0 all-to-all-done.1
  28.6 1.4 broadcast_in_dim.57
  30.0 6.0 %all-to-all-start = ((bf16[16,8,7168]{2,1,0:T(8,128)(2,1)}), bf16[16,8,7168]{2,1,0:T(8,128)(2,1)S(1)}, u32[]{:S(2)}, u32[]{:S(2)}) async-start(bf16[16,8,7168]{2,1,0:T(8,128)(2,1)} %bitcast.62), calls=%async_computation | async-start | bytes 3670016 | tf_op jit(solution)/shard_map/all_to_all | solution.py:56
  36.0 3.0 %concatenate.7 = bf16[129,7168]{1,0:T(8,128)(2,1)} pad(bf16[128,7168]{1,0:T(8,128)(2,1)} %param.8, bf16[]{:T(256)} %constant.14.clone.1), padding=0_1x0_0 | pad | bytes 3684354 | tf_op jit(solution)/shard_map/concatenate | solution.py:43
  39.0 3.0 %gather_fusion.1 = bf16[32,7168]{1,0:T(8,128)(2,1)S(1)} fusion(bf16[129,7168]{1,0:T(8,128)(2,1)} %concatenate.7, s32[1024]{0:T(1024)S(1)} %pad_clamp_fusion), kind=kCustom, calls=%fused_computation.1 | custom fusion | bytes 917632 | tf_op jit(solution)/shard_map/gather | solution.py:43
  42.0 37.8 %all-to-all-done = bf16[16,8,7168]{2,1,0:T(8,128)(2,1)S(1)} async-done(((bf16[16,8,7168]{2,1,0:T(8,128)(2,1)}), bf16[16,8,7168]{2,1,0:T(8,128)(2,1)S(1)}, u32[]{:S(2)}, u32[]{:S(2)}) %all-to-all-start) | async-done | bytes 1835040 | tf_op jit(solution)/shard_map/all_to_all | solution.py:56
  79.8 1.4 broadcast_in_dim.62
  81.2 4.4 %all-to-all-start.2 = ((bf16[16,8,7168]{2,1,0:T(8,128)(2,1)}), bf16[16,8,7168]{2,1,0:T(8,128)(2,1)}, u32[]{:S(2)}, u32[]{:S(2)}) async-start(bf16[16,8,7168]{2,1,0:T(8,128)(2,1)} %bitcast.61), calls=%async_computation.2 | async-start | bytes 3670016 | tf_op jit(solution)/shard_map/all_to_all | solution.py:59
  85.7 4.3 %scatter_custom_fusion.2 = s32[32]{0:T(128)S(1)} fusion(s32[1024]{0:T(1024)S(1)} %bitcast.71, s32[1024]{0:T(1024)S(1)} %iota.14, s32[]{:T(128)} %constant.45.clone.1), kind=kCustom, calls=%fused_computation.54 | custom fusion | bytes 132 | tf_op jit(solution)/shard_map/scatter | solution.py:32
  90.0 0.1 reshape.120
  90.1 0.0 copy-start
  90.1 2.8 %fusion.2 = f32[128,256]{1,0:T(8,128)S(1)} fusion(bf16[1,7168,256]{2,1,0:T(8,128)(2,1)} %param.11, bf16[16,8,7168]{2,1,0:T(8,128)(2,1)S(1)} %all-to-all-done), kind=kOutput, calls=%fused_computation.10 | convolution fusion | flops 469762048 | bytes 5636096 | tf_op jit(solution)/shard_map/dot_general | solution.py:69
  93.0 0.3 copy-done
  93.3 0.7 fusion.4
  93.9 35.5 %all-to-all-done.2 = bf16[16,8,7168]{2,1,0:T(8,128)(2,1)} async-done(((bf16[16,8,7168]{2,1,0:T(8,128)(2,1)}), bf16[16,8,7168]{2,1,0:T(8,128)(2,1)}, u32[]{:S(2)}, u32[]{:S(2)}) %all-to-all-start.2) | async-done | bytes 1835040 | tf_op jit(solution)/shard_map/all_to_all | solution.py:59
  129.5 4.0 %multiply_reduce_fusion = (f32[128]{0:T(128)S(1)}, f32[128,256]{1,0:T(8,128)S(1)}) fusion(f32[128,256]{1,0:T(8,128)S(1)} %fusion.4, f32[128,256]{1,0:T(8,128)S(1)} %fusion.2, bf16[1,256,7168]{2,1,0:T(8,128)(2,1)} %param.13, bf16[16,8,7168]{2,1,0:T(8,128)(2,1)} %all-to-all-done.2), kind=kOutput, calls=%fused_computation.21 | convolution fusion | flops 469991296 | bytes 5898752 | tf_op jit(solution)/shard_map/dot_general | solution.py:71
  133.5 0.7 all_to_all.22
  134.2 3.7 %all-to-all-start.3 = ((f32[16,1,8]{2,1,0:T(1,128)}), f32[16,1,8]{2,1,0:T(1,128)S(1)}, u32[]{:S(2)}, u32[]{:S(2)}) async-start(f32[16,1,8]{2,1,0:T(1,128)} %bitcast.15), calls=%async_computation.3 | async-start | bytes 16384 | tf_op jit(solution)/shard_map/all_to_all | solution.py:90
  137.9 3.0 %fusion = bf16[1,7168,256]{2,1,0:T(8,128)(2,1)} fusion(bf16[16,8,7168]{2,1,0:T(8,128)(2,1)S(1)} %all-to-all-done, f32[128,256]{1,0:T(8,128)S(1)} %fusion.2, f32[128,256]{1,0:T(8,128)S(1)} %fusion.4, f32[128,256]{1,0:T(8,128)S(1)} %get-tuple-element.10, f32[128]{0:T(128)S(1)} %reshape.120), kind=kOutput, calls=%fused_computation.8 | convolution fusion | flops 471957504 | bytes 5898752 | tf_op jit(solution)/shard_map/dot_general | solution.py:83
  140.9 3.0 %fusion.1 = bf16[1,7168,256]{2,1,0:T(8,128)(2,1)} fusion(bf16[16,8,7168]{2,1,0:T(8,128)(2,1)S(1)} %all-to-all-done, f32[128,256]{1,0:T(8,128)S(1)} %get-tuple-element.10, f32[128]{0:T(128)S(1)} %reshape.120, f32[128,256]{1,0:T(8,128)S(1)} %fusion.2), kind=kOutput, calls=%fused_computation.9 | convolution fusion | flops 471826432 | bytes 5767680 | tf_op jit(solution)/shard_map/dot_general | solution.py:86
  143.9 0.1 all-to-all-done.3
  144.0 0.1 reshape.165
  144.1 0.7 scatter_custom_fusion.3
  144.8 0.1 reshape.119
  144.9 0.7 copy.23
  (11 shorter events, 0.1 us)
Async XLA Ops:
  14.3 14.3 %all-to-all-start.1 = ((bf16[16,1,8]{2,1,0:T(2,128)(2,1)}), bf16[16,1,8]{2,1,0:T(2,128)(2,1)S(1)}, u32[]{:S(2)}, u32[]{:S(2)}) async-start(bf16[16,1,8]{2,1,0:T(2,128)(2,1)} %copy.21), calls=%async_computation.1 | async-start | bytes 16384 | tf_op jit(solution)/shard_map/all_to_all | solution.py:62
  30.0 49.8 %all-to-all-start = ((bf16[16,8,7168]{2,1,0:T(8,128)(2,1)}), bf16[16,8,7168]{2,1,0:T(8,128)(2,1)S(1)}, u32[]{:S(2)}, u32[]{:S(2)}) async-start(bf16[16,8,7168]{2,1,0:T(8,128)(2,1)} %bitcast.62), calls=%async_computation | async-start | bytes 3670016 | tf_op jit(solution)/shard_map/all_to_all | solution.py:56
  81.2 48.2 %all-to-all-start.2 = ((bf16[16,8,7168]{2,1,0:T(8,128)(2,1)}), bf16[16,8,7168]{2,1,0:T(8,128)(2,1)}, u32[]{:S(2)}, u32[]{:S(2)}) async-start(bf16[16,8,7168]{2,1,0:T(8,128)(2,1)} %bitcast.61), calls=%async_computation.2 | async-start | bytes 3670016 | tf_op jit(solution)/shard_map/all_to_all | solution.py:59
  90.1 3.1 %copy-start = (bf16[1,7168,256]{2,1,0:T(8,128)(2,1)S(1)}, bf16[1,7168,256]{2,1,0:T(8,128)(2,1)}, u32[]{:S(2)}) copy-start(bf16[1,7168,256]{2,1,0:T(8,128)(2,1)} %param.12) | copy-start | bytes 11010052
  134.2 9.8 %all-to-all-start.3 = ((f32[16,1,8]{2,1,0:T(1,128)}), f32[16,1,8]{2,1,0:T(1,128)S(1)}, u32[]{:S(2)}, u32[]{:S(2)}) async-start(f32[16,1,8]{2,1,0:T(1,128)} %bitcast.15), calls=%async_computation.3 | async-start | bytes 16384 | tf_op jit(solution)/shard_map/all_to_all | solution.py:90
where the time goes:
time: 146 us
  waiting for transfers between devices  73.4 us (50%)
  local copies, waits for them, and re-layouts  33.3 us (23%)
  starting transfers between devices  21.5 us (15%)
  matrix products  13.6 us (9%)
  other arithmetic  2.9 us (2%)
    all_to_all x1, waiting for transfers between devices, local(): lax.all_to_all(widen_rows(send_rows), ('expert', 'dp'), split_axis=0, con...  37.8 us
    all_to_all x1, waiting for transfers between devices, local(): lax.all_to_all(widen_rows(send_cots), ('expert', 'dp'), split_axis=0, con...  35.5 us
    scatter x1, local copies, waits for them, and re-layouts, local(): weight_table = jnp.zeros((expert_count * CAP,), jnp.bfloat16).at[target]....  7.58 us
    all_to_all x1, starting transfers between devices, local(): lax.all_to_all(widen_rows(send_weight), ('expert', 'dp'), split_axis=0, c...  7.39 us
    all_to_all x1, starting transfers between devices, local(): lax.all_to_all(widen_rows(send_rows), ('expert', 'dp'), split_axis=0, con...  6 us
    all_to_all x1, starting transfers between devices, local(): lax.all_to_all(widen_rows(send_cots), ('expert', 'dp'), split_axis=0, con...  4.41 us
    scatter x1, local copies, waits for them, and re-layouts, local(): slot_table = jnp.full((expert_count * CAP,), slot_count, jnp.int32).at[ta...  4.3 us
    scatter x1, local copies, waits for them, and re-layouts, local(): token_table = jnp.full((expert_count * CAP,), tok_count, jnp.int32).at[ta...  4.3 us
  transfers between devices with their start and end apart: 4, of which 3 were waited for; matrix products, arithmetic and copies ran while one was open for 18% of the time, Pallas kernels for 0%

commit v1 on v0

v1 whole, which is shorter than its diff:
```python
import jax
import jax.numpy as jnp
from jax import lax
from jax.sharding import PartitionSpec as P

CAP = 8


def dot_first(a, b):
    return lax.dot_general(a, b, (((0,), (0,)), ((), ())), preferred_element_type=jnp.float32)


def general(tokens, cotangent, route_ids, route_weight, gate_weight, up_weight, down_weight):
    expert_count = lax.axis_size("expert")
    dp_count = lax.axis_size("dp")
    tok_count, model_width = tokens.shape
    experts = jnp.arange(expert_count, dtype=jnp.int32)
    hit = route_ids[:, :, None] == experts[None, None, :]
    chosen = jnp.any(hit, axis=1)
    weight_tok = jnp.sum(jnp.where(hit, route_weight.astype(jnp.float32)[:, :, None], 0.0), axis=1)
    row = jnp.arange(tok_count, dtype=jnp.int32)
    earlier = (row[None, :] < row[:, None]).astype(jnp.bfloat16)
    rank = jnp.dot(earlier, chosen.astype(jnp.bfloat16), preferred_element_type=jnp.float32).astype(jnp.int32)
    place = jnp.arange(CAP, dtype=jnp.int32)
    select = chosen[:, :, None] & (rank[:, :, None] == place[None, None, :])
    onehot = select.reshape(tok_count, expert_count * CAP).astype(jnp.bfloat16)
    send_weight = jnp.sum(jnp.where(select, weight_tok[:, :, None], 0.0), axis=0).astype(jnp.bfloat16)
    send_rows = dot_first(onehot, tokens).astype(jnp.bfloat16).reshape(expert_count, CAP, model_width)
    send_cots = dot_first(onehot, cotangent).astype(jnp.bfloat16).reshape(expert_count, CAP, model_width)

    def widen_rows(array):
        spread = jnp.broadcast_to(array[:, None], (expert_count, dp_count) + array.shape[1:])
        return spread.reshape((expert_count * dp_count,) + array.shape[1:])

    def exchange(array):
        return lax.all_to_all(array, ("expert", "dp"), split_axis=0, concat_axis=0, tiled=True)

    row_block = exchange(widen_rows(send_rows)).reshape(-1, model_width)
    cot_block = exchange(widen_rows(send_cots)).reshape(-1, model_width)
    weights = exchange(widen_rows(send_weight)).reshape(-1).astype(jnp.float32)
    gate_pre = jnp.dot(row_block, gate_weight[0], preferred_element_type=jnp.float32)
    up_pre = jnp.dot(row_block, up_weight[0], preferred_element_type=jnp.float32)
    back_proj = lax.dot_general(
        cot_block, down_weight[0], (((1,), (1,)), ((), ())), preferred_element_type=jnp.float32
    )
    gate_sig = jax.nn.sigmoid(gate_pre)
    gate_act = gate_pre * gate_sig
    partial = jnp.sum(gate_act * up_pre * back_proj, axis=1).reshape(expert_count * dp_count, CAP)
    act_grad = weights[:, None] * back_proj
    d_gate = (act_grad * up_pre * gate_sig * (1.0 + gate_pre * (1.0 - gate_sig))).astype(jnp.bfloat16)
    d_up = (act_grad * gate_act).astype(jnp.bfloat16)
    grad_gate = dot_first(row_block, d_gate).astype(jnp.bfloat16)
    grad_up = dot_first(row_block, d_up).astype(jnp.bfloat16)
    returned = exchange(partial)
    slot_sums = jnp.sum(returned.reshape(expert_count, dp_count, CAP), axis=1)
    value = jnp.sum(jnp.where(select, slot_sums[None], 0.0), axis=2)
    route_grad = jnp.sum(jnp.where(hit, value[:, None, :], 0.0), axis=2)
    return grad_gate[None], grad_up[None], route_grad


def solution(mesh):
    return jax.shard_map(
        general,
        mesh=mesh,
        in_specs=(
            P(("groups", "expert", "dp"), None),
            P(("groups", "expert", "dp"), None),
            P(("groups", "expert", "dp"), None),
            P(("groups", "expert", "dp"), None),
            P("expert", None, "dp"),
            P("expert", None, "dp"),
            P("expert", "dp", None),
        ),
        out_specs=(
            P(("groups", "expert"), None, "dp"),
            P(("groups", "expert"), None, "dp"),
            P(("groups", "expert", "dp"), None),
        ),
        check_vma=False,
    )
```

time: 146 us -> 139 us (0.952)
  local copies, waits for them, and re-layouts: 33.3 us -> 4.44 us
  waiting for transfers between devices: 73.4 us -> 86.1 us
  blocking collectives: 0 us -> 8.93 us
  matrix products: 13.6 us -> 21.1 us
  starting transfers between devices: 21.5 us -> 15.3 us
    scatter x4 -> x0, local copies, waits for them, and re-layouts: 16.9 us -> none  [the longest x1 7.58 us: local(): weight_table = jnp.zeros((expert_count * CAP,), jnp.bfloat16).at[target]....]
    all_to_all x4 -> x3, waiting for transfers between devices: 73.4 us -> 86.1 us  [exchange(): lax.all_to_all(array, ('expert', 'dp'), split_axis=0, concat_axis=0, tile...]
    all_to_all x0 -> x1, blocking collectives: none -> 8.93 us  [exchange(): lax.all_to_all(array, ('expert', 'dp'), split_axis=0, concat_axis=0, tile...]
    dot_general x5 -> x8, matrix products: 13.6 us -> 21.1 us  [the longest x4 11.4 us: dot_first(): lax.dot_general(a, b, (((0,), (0,)), ((), ())), preferred_element_type=jn...]
    all_to_all x4 -> x3, starting transfers between devices: 21.5 us -> 15.3 us  [exchange(): lax.all_to_all(array, ('expert', 'dp'), split_axis=0, concat_axis=0, tile...]
    concatenate x2 -> x0, local copies, waits for them, and re-layouts: 4.63 us -> none  [the longest x1 2.95 us: local(): jnp.concatenate([cotangent, blank_row], axis=0)[token_table]]
    gather x2 -> x0, local copies, waits for them, and re-layouts: 3.87 us -> none  [the longest x1 3.04 us: local(): jnp.concatenate([cotangent, blank_row], axis=0)[token_table]]
    unnamed x5 -> x8, local copies, waits for them, and re-layouts: 2.54 us -> 0.73 us
  transfers between devices with their start and end apart: 4 -> 3, of which waited for: 3 -> 3; matrix products, arithmetic and copies ran while one was open for 18% -> 5% of each run, Pallas kernels for 0% -> 0%
where the time goes in v1:
time: 139 us; the launch traced here: 138 us
  waiting for transfers between devices  86.1 us (62%)
  matrix products  21.1 us (15%)
  starting transfers between devices  15.3 us (11%)
  blocking collectives  8.93 us (6%)
  local copies, waits for them, and re-layouts  4.44 us (3%)
  other arithmetic  1.67 us (1%)
    all_to_all x3, waiting for transfers between devices, exchange(): lax.all_to_all(array, ('expert', 'dp'), split_axis=0, concat_axis=0, tile...  86.1 us
    all_to_all x3, starting transfers between devices, exchange(): lax.all_to_all(array, ('expert', 'dp'), split_axis=0, concat_axis=0, tile...  15.3 us
    dot_general x4, matrix products, dot_first(): lax.dot_general(a, b, (((0,), (0,)), ((), ())), preferred_element_type=jn...  11.4 us
    all_to_all x1, blocking collectives, exchange(): lax.all_to_all(array, ('expert', 'dp'), split_axis=0, concat_axis=0, tile...  8.93 us
    dot_general x1, matrix products, general(): lax.dot_general(cot_block, down_weight[0], (((1,), (1,)), ((), ())), pref...  4.02 us
    dot_general x1, matrix products, general(): jnp.dot(row_block, gate_weight[0], preferred_element_type=jnp.float32)  3.39 us
    broadcast_in_dim x3, local copies, waits for them, and re-layouts, widen_rows(): jnp.broadcast_to(array[:, None], (expert_count, dp_count) + array.shape[1:])  2.83 us
  transfers between devices with their start and end apart: 3, of which 3 were waited for; matrix products, arithmetic and copies ran while one was open for 5% of the time, Pallas kernels for 0%

profile of v1, /device:TPU:0, one launch (start us, length us, event | category | flops | bytes accessed | tf_op | source)
XLA Modules:
  0.0 138.3 jit_solution(15641795301688288879)
XLA Ops:
  0.6 0.0 copy-start
  0.6 0.8 fusion.20
  1.5 0.1 convolution_convert_fusion.4
  1.6 0.1 eq.43
  1.7 0.4 copy-done
  2.2 0.4 fusion.2
  2.6 1.4 %broadcast_in_dim.83 = bf16[4,4,8,7168]{3,2,1,0:T(8,128)(2,1)} broadcast(bf16[4,8,7168]{2,1,0:T(8,128)(2,1)S(1)} %fusion.2), dimensions={0,2,3} | broadcast | bytes 2293760 | tf_op jit(solution)/shard_map/broadcast_in_dim | solution.py:32
  4.0 7.4 %all-to-all-start = ((bf16[16,8,7168]{2,1,0:T(8,128)(2,1)}), bf16[16,8,7168]{2,1,0:T(8,128)(2,1)}, u32[]{:S(2)}, u32[]{:S(2)}) async-start(bf16[16,8,7168]{2,1,0:T(8,128)(2,1)} %bitcast.51), calls=%async_computation | async-start | bytes 3670016 | tf_op jit(solution)/shard_map/all_to_all | solution.py:36
  11.4 1.9 %fusion.3 = bf16[4,8,7168]{2,1,0:T(8,128)(2,1)S(1)} fusion(bf16[128,7168]{1,0:T(8,128)(2,1)} %param.8, s32[32]{0:T(128)S(1)} %eq.43, s32[128,4]{0,1:T(4,128)S(1)} %convolution_convert_fusion.4, pred[128,4]{0,1:T(4,128)(4,1)S(1)} %fusion.20), kind=kOutput, calls=%fused_computation.7 | convolution fusion | flops 58957824 | bytes 2296448 | tf_op jit(solution)/shard_map/dot_general | solution.py:10
  13.3 42.0 %all-to-all-done = bf16[16,8,7168]{2,1,0:T(8,128)(2,1)} async-done(((bf16[16,8,7168]{2,1,0:T(8,128)(2,1)}), bf16[16,8,7168]{2,1,0:T(8,128)(2,1)}, u32[]{:S(2)}, u32[]{:S(2)}) %all-to-all-start) | async-done | bytes 1835040 | tf_op jit(solution)/shard_map/all_to_all | solution.py:36
  55.3 1.4 %broadcast_in_dim.90 = bf16[4,4,8,7168]{3,2,1,0:T(8,128)(2,1)} broadcast(bf16[4,8,7168]{2,1,0:T(8,128)(2,1)S(1)} %fusion.3), dimensions={0,2,3} | broadcast | bytes 2293760 | tf_op jit(solution)/shard_map/broadcast_in_dim | solution.py:32
  56.7 4.4 %all-to-all-start.2 = ((bf16[16,8,7168]{2,1,0:T(8,128)(2,1)}), bf16[16,8,7168]{2,1,0:T(8,128)(2,1)}, u32[]{:S(2)}, u32[]{:S(2)}) async-start(bf16[16,8,7168]{2,1,0:T(8,128)(2,1)} %bitcast.52), calls=%async_computation.2 | async-start | bytes 3670016 | tf_op jit(solution)/shard_map/all_to_all | solution.py:36
  61.1 0.0 copy-start.1
  61.1 3.4 %fusion.4 = f32[128,256]{1,0:T(8,128)S(1)} fusion(bf16[1,7168,256]{2,1,0:T(8,128)(2,1)} %param.11, bf16[16,8,7168]{2,1,0:T(8,128)(2,1)} %all-to-all-done), kind=kOutput, calls=%fused_computation.8 | convolution fusion | flops 469762048 | bytes 5636096 | tf_op jit(solution)/shard_map/dot_general | solution.py:41
  64.5 0.3 copy-done.1
  64.8 2.2 %fusion.6 = f32[128,256]{1,0:T(8,128)S(1)} fusion(bf16[1,7168,256]{2,1,0:T(8,128)(2,1)S(1)} %copy-done.1, bf16[16,8,7168]{2,1,0:T(8,128)(2,1)} %all-to-all-done), kind=kOutput, calls=%fused_computation.10 | convolution fusion | flops 469762048 | bytes 5636096 | tf_op jit(solution)/shard_map/dot_general | solution.py:42
  67.0 0.0 copy-start.3
  67.0 0.0 copy-start.2
  67.0 37.9 %all-to-all-done.2 = bf16[16,8,7168]{2,1,0:T(8,128)(2,1)} async-done(((bf16[16,8,7168]{2,1,0:T(8,128)(2,1)}), bf16[16,8,7168]{2,1,0:T(8,128)(2,1)}, u32[]{:S(2)}, u32[]{:S(2)}) %all-to-all-start.2) | async-done | bytes 1835040 | tf_op jit(solution)/shard_map/all_to_all | solution.py:36
  105.0 4.0 %multiply_reduce_fusion = (f32[128]{0:T(128)S(1)}, f32[128,256]{1,0:T(8,128)S(1)}) fusion(f32[128,256]{1,0:T(8,128)S(1)} %fusion.6, f32[128,256]{1,0:T(8,128)S(1)} %fusion.4, bf16[1,256,7168]{2,1,0:T(8,128)(2,1)} %param.13, bf16[16,8,7168]{2,1,0:T(8,128)(2,1)} %all-to-all-done.2), kind=kOutput, calls=%fused_computation.20 | convolution fusion | flops 469991296 | bytes 5898752 | tf_op jit(solution)/shard_map/dot_general | solution.py:43
  109.0 0.7 all_to_all.22
  109.7 3.5 %all-to-all-start.3 = ((f32[16,1,8]{2,1,0:T(1,128)}), f32[16,1,8]{2,1,0:T(1,128)S(1)}, u32[]{:S(2)}, u32[]{:S(2)}) async-start(f32[16,1,8]{2,1,0:T(1,128)} %bitcast.14), calls=%async_computation.3 | async-start | bytes 16384 | tf_op jit(solution)/shard_map/all_to_all | solution.py:36
  113.1 0.0 copy-done.3
  113.2 6.2 %all-to-all-done.3 = f32[16,1,8]{2,1,0:T(1,128)S(1)} async-done(((f32[16,1,8]{2,1,0:T(1,128)}), f32[16,1,8]{2,1,0:T(1,128)S(1)}, u32[]{:S(2)}, u32[]{:S(2)}) %all-to-all-start.3) | async-done | bytes 544 | tf_op jit(solution)/shard_map/all_to_all | solution.py:36
  119.4 0.1 select_reduce_fusion.1
  119.5 0.0 copy-done.2
  119.5 0.6 select_reduce_fusion
  120.1 0.1 select_reduce_fusion.2
  120.2 8.9 %all_to_all.28 = bf16[16,1,8]{2,1,0:T(2,128)(2,1)S(1)} all-to-all(bf16[16,1,8]{2,1,0:T(2,128)(2,1)S(1)} %copy.20), channel_id=1, replica_groups=mesh['groups'=2,'expert'=4,'dp'=4] {'expert','dp'}, dimensions={0} | all-to-all | bytes 512 | tf_op jit(solution)/shard_map/all_to_all | solution.py:36
  129.2 0.1 reshape.60
  129.3 4.5 %fusion = bf16[1,7168,256]{2,1,0:T(8,128)(2,1)} fusion(bf16[16,8,7168]{2,1,0:T(8,128)(2,1)} %all-to-all-done, f32[128,256]{1,0:T(8,128)S(1)} %fusion.4, f32[128,256]{1,0:T(8,128)S(1)} %fusion.6, f32[128,256]{1,0:T(8,128)S(1)} %get-tuple-element.6, f32[128]{0:T(128)S(1)} %reshape.60), kind=kOutput, calls=%fused_computation.2 | convolution fusion | flops 471957504 | bytes 5898752 | tf_op jit(solution)/shard_map/dot_general | solution.py:10
  133.8 4.5 %fusion.1 = bf16[1,7168,256]{2,1,0:T(8,128)(2,1)} fusion(bf16[16,8,7168]{2,1,0:T(8,128)(2,1)} %all-to-all-done, f32[128,256]{1,0:T(8,128)S(1)} %get-tuple-element.6, f32[128]{0:T(128)S(1)} %reshape.60, f32[128,256]{1,0:T(8,128)S(1)} %fusion.4), kind=kOutput, calls=%fused_computation.3 | convolution fusion | flops 471826432 | bytes 5767680 | tf_op jit(solution)/shard_map/dot_general | solution.py:10
  (6 shorter events, 0.1 us)
Async XLA Ops:
  0.6 1.5 %copy-start = (bf16[128,7168]{1,0:T(8,128)(2,1)S(1)}, bf16[128,7168]{1,0:T(8,128)(2,1)}, u32[]{:S(2)}) copy-start(bf16[128,7168]{1,0:T(8,128)(2,1)} %param.7) | copy-start | bytes 5505028
  4.0 51.3 %all-to-all-start = ((bf16[16,8,7168]{2,1,0:T(8,128)(2,1)}), bf16[16,8,7168]{2,1,0:T(8,128)(2,1)}, u32[]{:S(2)}, u32[]{:S(2)}) async-start(bf16[16,8,7168]{2,1,0:T(8,128)(2,1)} %bitcast.51), calls=%async_computation | async-start | bytes 3670016 | tf_op jit(solution)/shard_map/all_to_all | solution.py:36
  56.7 48.2 %all-to-all-start.2 = ((bf16[16,8,7168]{2,1,0:T(8,128)(2,1)}), bf16[16,8,7168]{2,1,0:T(8,128)(2,1)}, u32[]{:S(2)}, u32[]{:S(2)}) async-start(bf16[16,8,7168]{2,1,0:T(8,128)(2,1)} %bitcast.52), calls=%async_computation.2 | async-start | bytes 3670016 | tf_op jit(solution)/shard_map/all_to_all | solution.py:36
  61.1 3.7 %copy-start.1 = (bf16[1,7168,256]{2,1,0:T(8,128)(2,1)S(1)}, bf16[1,7168,256]{2,1,0:T(8,128)(2,1)}, u32[]{:S(2)}) copy-start(bf16[1,7168,256]{2,1,0:T(8,128)(2,1)} %param.12) | copy-start | bytes 11010052
  67.0 46.2 %copy-start.3 = (bf16[128,8]{0,1:T(8,128)(2,1)S(1)}, bf16[128,8]{0,1:T(8,128)(2,1)}, u32[]{:S(2)}) copy-start(bf16[128,8]{0,1:T(8,128)(2,1)} %param.10) | copy-start | bytes 6148
  67.0 52.5 %copy-start.2 = (s32[128,8]{0,1:T(8,128)S(1)}, s32[128,8]{0,1:T(8,128)}, u32[]{:S(2)}) copy-start(s32[128,8]{0,1:T(8,128)} %param.9) | copy-start | bytes 12292
  109.7 9.7 %all-to-all-start.3 = ((f32[16,1,8]{2,1,0:T(1,128)}), f32[16,1,8]{2,1,0:T(1,128)S(1)}, u32[]{:S(2)}, u32[]{:S(2)}) async-start(f32[16,1,8]{2,1,0:T(1,128)} %bitcast.14), calls=%async_computation.3 | async-start | bytes 16384 | tf_op jit(solution)/shard_map/all_to_all | solution.py:36

commit v2 on v1

--- a/solution.py
+++ b/solution.py
@@ -1,6 +1,11 @@
+import functools
+import math
+
 import jax
 import jax.numpy as jnp
 from jax import lax
+from jax.experimental import pallas as pl
+from jax.experimental.pallas import tpu as pltpu
 from jax.sharding import PartitionSpec as P
 
 CAP = 8
@@ -58,9 +63,357 @@
     return grad_gate[None], grad_up[None], route_grad
 
 
+PAIR = 2
+
+
+def move_kernel(
+    shape, ids_ref, rw_ref, tok_hbm, cot_hbm, wg_hbm, wu_hbm, wd_hbm,
+    rows_ref, dcat_ref, grad_ref,
+    cots_ref, tok_ref, cot_ref, wg_ref, wu_ref, wd_ref, st_ref, sc_ref, pbuf, rbuf,
+    load_sem, y_sem, up_sem, down_sem, core_sem, recv_sem, back_sem, home_sem,
+):
+    y_count, z_count, cap = shape
+    width = tok_ref.shape[1]
+    hidden = wg_ref.shape[1]
+    toks = tok_ref.shape[0]
+    chunk = math.gcd(width, 1024)
+    me = lax.axis_index("expert")
+    z = lax.axis_index("dp")
+    y, c = lax.div(me, PAIR), lax.rem(me, PAIR)
+    slots = y_count * cap
+    plane = PAIR * slots
+
+    loads = [
+        pltpu.make_async_copy(src, dst, load_sem.at[i])
+        for i, (src, dst) in enumerate(
+            ((tok_hbm, tok_ref), (cot_hbm, cot_ref), (wg_hbm, wg_ref), (wu_hbm, wu_ref), (wd_hbm, wd_ref))
+        )
+    ]
+    for load in loads:
+        load.start()
+
+    group = PAIR * y_count * z_count
+    mine = me * z_count + z
+
+    def place_of(index):
+        return {"expert": lax.div(index, z_count), "dp": lax.rem(index, z_count)}
+
+    barrier = pltpu.get_barrier_semaphore()
+    for step in range(1, group):
+        pl.semaphore_signal(
+            barrier, inc=1, device_id=place_of(lax.rem(mine + step, group)), device_id_type=pl.DeviceIdType.MESH
+        )
+
+    ids = ids_ref[...]
+    rw = rw_ref[...].astype(jnp.float32)
+    experts = PAIR * y_count
+    padded = -(-experts // 16) * 16
+    number = lax.broadcasted_iota(jnp.int32, (padded, toks), 0)
+    chosen = jnp.zeros((padded, toks), jnp.float32)
+    for k in range(ids.shape[0]):
+        chosen += jnp.where(ids[k : k + 1, :] == number, 1.0, 0.0)
+    earlier = lax.broadcasted_iota(jnp.int32, (toks, toks), 0) < lax.broadcasted_iota(jnp.int32, (toks, toks), 1)
+    upper = jnp.where(earlier, 1.0, 0.0).astype(jnp.bfloat16)
+    rank = jnp.dot(chosen.astype(jnp.bfloat16), upper, preferred_element_type=jnp.float32)
+    total = jnp.sum(chosen, axis=1, keepdims=True)
+    slot = lax.broadcasted_iota(jnp.int32, (slots, toks), 0).astype(jnp.float32)
+    lane = lax.broadcasted_iota(jnp.int32, (slots, 128), 1)
+    select = jnp.zeros((slots, toks), jnp.float32)
+    tail = jnp.zeros((slots, 128), jnp.float32)
+    picks = []
+    for e in range(experts):
+        spot = rank[e : e + 1, :] + float((e // PAIR) * cap)
+        if e % PAIR:
+            spot = spot + total[e - 1 : e, :]
+        pick = jnp.where((slot == spot) & (chosen[e : e + 1, :] > 0.5), 1.0, 0.0)
+        weight = jnp.sum(jnp.where(ids == e, rw, 0.0), axis=0, keepdims=True)
+        tail += jnp.where(lane == e % PAIR, jnp.sum(pick * weight, axis=1, keepdims=True), 0.0)
+        select += pick
+        picks.append(pick)
+    select = select.astype(jnp.bfloat16)
+
+    def row_of(z_src, c_src, y_src):
+        return pl.multiple_of(((z_src * PAIR + c_src) * y_count + y_src) * cap, cap)
+
+    def block(kind, z_src, c_src, y_src):
+        ref = rows_ref if kind == 0 else cots_ref
+        return ref.at[pl.ds(row_of(z_src, c_src, y_src), cap), :]
+
+    def remote(kind, z_src, c_src, y_src, send_sem, target, src=None):
+        there = block(kind, z_src, c_src, y_src)
+        return pltpu.make_async_remote_copy(
+            src_ref=there if src is None else src,
+            dst_ref=there,
+            send_sem=send_sem,
+            recv_sem=recv_sem.at[z_src, c_src, y_src, kind],
+            device_id=target,
+            device_id_type=pl.DeviceIdType.MESH,
+        )
+
+    def to_up(kind, z_src, y_src):
+        return remote(kind, z_src, c, y_src, up_sem.at[z_src, y_src, kind], {"dp": z + 1})
+
+    def to_down(kind, z_src, y_src):
+        return remote(kind, z_src, c, y_src, down_sem.at[z_src, y_src, kind], {"dp": z - 1})
+
+    def to_core(kind, z_src, y_src):
+        return remote(kind, z_src, c, y_src, core_sem.at[z_src, y_src, kind], {"expert": y * PAIR + 1 - c})
+
+    def to_y(kind, step):
+        y_to = lax.rem(y + step, y_count)
+        ref = st_ref if kind == 0 else sc_ref
+        src = ref.at[pl.ds(pl.multiple_of(y_to * cap, cap), cap), :]
+        return remote(kind, z, c, y, y_sem.at[step, kind], {"expert": y_to * PAIR + c}, src)
+
+    def arrived(kind, z_src, c_src, y_src):
+        there = block(kind, z_src, c_src, y_src)
+        pltpu.make_async_remote_copy(
+            src_ref=there, dst_ref=there, send_sem=load_sem.at[0], recv_sem=recv_sem.at[z_src, c_src, y_src, kind],
+            device_id={"expert": y * PAIR + 1 - c}, device_id_type=pl.DeviceIdType.MESH,
+        ).wait_recv()
+
+    def spread(kind, y_src):
+        @pl.when(z + 1 < z_count)
+        def _():
+            to_up(kind, z, y_src).start()
+
+        @pl.when(z > 0)
+        def _():
+            to_down(kind, z, y_src).start()
+
+        to_core(kind, z, y_src).start()
+
+    own = pl.ds(pl.multiple_of(y * cap, cap), cap)
+    for kind, (load, src, out) in enumerate(((loads[0], tok_ref, st_ref), (loads[1], cot_ref, sc_ref))):
+        load.wait()
+
+        @pl.loop(0, width // chunk)
+        def _(i, src=src, out=out):
+            at = pl.ds(pl.multiple_of(i * chunk, chunk), chunk)
+            out[:, at] = jnp.dot(select, src[:, at], preferred_element_type=jnp.float32).astype(jnp.bfloat16)
+
+        if kind == 0:
+            st_ref[:, width:] = tail.astype(jnp.bfloat16)
+            pl.semaphore_wait(barrier, group - 1)
+        for step in range(1, y_count):
+            to_y(kind, step).start()
+        (rows_ref if kind == 0 else cots_ref)[pl.ds(row_of(z, c, y), cap), :] = out[own, :]
+        spread(kind, y)
+    for kind in range(2):
+        for step in range(1, y_count):
+            y_src = lax.rem(y + y_count - step, y_count)
+            arrived(kind, z, c, y_src)
+            spread(kind, y_src)
+
+    def forward(z_src):
+        for kind in range(2):
+            for y_src in range(y_count):
+                arrived(kind, z_src, 1 - c, y_src)
+        rows = pl.ds(pl.multiple_of(z_src * plane, plane), plane)
+
+        def add(i, sums):
+            at = pl.ds(pl.multiple_of(i * chunk, chunk), chunk)
+            x, t = rows_ref[rows, at], cots_ref[rows, at]
+            return (
+                sums[0] + jnp.dot(x, wg_ref[at, :], preferred_element_type=jnp.float32),
+                sums[1] + jnp.dot(x, wu_ref[at, :], preferred_element_type=jnp.float32),
+                sums[2]
+                + lax.dot_general(t, wd_ref[:, at], (((1,), (1,)), ((), ())), preferred_element_type=jnp.float32),
+            )
+
+        zero = jnp.zeros((plane, hidden), jnp.float32)
+        gate_pre, up_pre, back = lax.fori_loop(0, width // chunk, add, (zero, zero, zero))
+        sig = jax.nn.sigmoid(gate_pre)
+        act = gate_pre * sig
+        part = jnp.sum(act * up_pre * back, axis=1, keepdims=True)
+        pbuf[rows, :] = jnp.broadcast_to(part, (plane, 128))
+        marks = rows_ref[rows, width:].astype(jnp.float32)
+        which = lax.broadcasted_iota(jnp.int32, (plane, 128), 1)
+        weight = jnp.sum(jnp.where(which == c, marks, 0.0), axis=1, keepdims=True)
+        act_grad = weight * back
+        dcat_ref[rows, :hidden] = (act_grad * up_pre * sig * (1.0 + gate_pre * (1.0 - sig))).astype(jnp.bfloat16)
+        dcat_ref[rows, hidden:] = (act_grad * act).astype(jnp.bfloat16)
+
+    def home(z_to, c_to, y_to):
+        return pltpu.make_async_remote_copy(
+            src_ref=pbuf.at[pl.ds(row_of(z_to, c_to, y_to), cap), :],
+            dst_ref=rbuf.at[pl.ds(pl.multiple_of(mine * cap, cap), cap), :],
+            send_sem=back_sem.at[z_to, c_to, y_to],
+            recv_sem=home_sem.at[mine],
+            device_id={"expert": y_to * PAIR + c_to, "dp": z_to},
+            device_id_type=pl.DeviceIdType.MESH,
+        )
+
+    def not_me(z_to, c_to, y_to):
+        return (z_to != z) | (c_to != c) | (y_to != y)
+
+    def go_home(z_to):
+        for c_to in range(PAIR):
+            for y_to in range(y_count):
+
+                @pl.when(not_me(z_to, c_to, y_to))
+                def _(c_to=c_to, y_to=y_to):
+                    home(z_to, c_to, y_to).start()
+
+    for load in loads[2:]:
+        load.wait()
+    for hop in range(1, z_count):
+        for kind in range(2):
+            for step in range(y_count):
+                y_src = lax.rem(y + y_count - step, y_count)
+
+                @pl.when(z >= hop)
+                def _(kind=kind, y_src=y_src, hop=hop):
+                    arrived(kind, z - hop, c, y_src)
+
+                    @pl.when(z + 1 < z_count)
+                    def _():
+                        to_up(kind, z - hop, y_src).start()
+
+                    to_core(kind, z - hop, y_src).start()
+
+                @pl.when(z + hop < z_count)
+                def _(kind=kind, y_src=y_src, hop=hop):
+                    arrived(kind, z + hop, c, y_src)
+
+                    @pl.when(z > 0)
+                    def _():
+                        to_down(kind, z + hop, y_src).start()
+
+                    to_core(kind, z + hop, y_src).start()
+
+            if kind == 0:
+                if hop == 1:
+                    forward(z)
+                    go_home(z)
+                else:
+
+                    @pl.when(z >= hop - 1)
+                    def _(hop=hop):
+                        forward(z - (hop - 1))
+                        go_home(z - (hop - 1))
+
+                    @pl.when(z + hop - 1 < z_count)
+                    def _(hop=hop):
+                        forward(z + (hop - 1))
+                        go_home(z + (hop - 1))
+
+    last = z_count - 1
+    if last == 0:
+        forward(z)
+        go_home(z)
+    else:
+
+        @pl.when(z >= last)
+        def _():
+            forward(z - last)
+            go_home(z - last)
+
+        @pl.when(z + last < z_count)
+        def _():
+            forward(z + last)
+            go_home(z + last)
+
+    rbuf[pl.ds(pl.multiple_of(mine * cap, cap), cap), :] = pbuf[pl.ds(row_of(z, c, y), cap), :]
+
+    for kind in range(2):
+        for step in range(1, y_count):
+            to_y(kind, step).wait_send()
+        for z_src in range(z_count):
+            for y_src in range(y_count):
+                to_core(kind, z_src, y_src).wait_send()
+
+                @pl.when((z_src <= z) & (z + 1 < z_count))
+                def _(kind=kind, z_src=z_src, y_src=y_src):
+                    to_up(kind, z_src, y_src).wait_send()
+
+                @pl.when((z_src >= z) & (z > 0))
+                def _(kind=kind, z_src=z_src, y_src=y_src):
+                    to_down(kind, z_src, y_src).wait_send()
+
+    for z_to in range(z_count):
+        for c_to in range(PAIR):
+            for y_to in range(y_count):
+
+                @pl.when(not_me(z_to, c_to, y_to))
+                def _(z_to=z_to, c_to=c_to, y_to=y_to):
+                    home(z_to, c_to, y_to).wait_send()
+                    spot = (y_to * PAIR + c_to) * z_count + z_to
+                    there = rbuf.at[pl.ds(spot * cap, cap), :]
+                    pltpu.make_async_remote_copy(
+                        src_ref=there, dst_ref=there, send_sem=load_sem.at[0], recv_sem=home_sem.at[spot],
+                        device_id={"expert": y * PAIR + 1 - c}, device_id_type=pl.DeviceIdType.MESH,
+                    ).wait_recv()
+
+    result = jnp.zeros(ids.shape, jnp.float32)
+    for e in range(experts):
+        first = e * z_count * cap
+        sums = rbuf[first : first + cap, :]
+        for k in range(1, z_count):
+            sums = sums + rbuf[first + k * cap : first + (k + 1) * cap, :]
+        pick = picks[e][(e // PAIR) * cap : (e // PAIR + 1) * cap, :]
+        value = jnp.sum(pick * sums, axis=0, keepdims=True)
+        result += jnp.where(ids == e, value, 0.0)
+    grad_ref[...] = result
+
+
+def moved(tokens, cotangent, route_ids, route_weight, gate_weight, up_weight, down_weight):
+    y_count = lax.axis_size("expert") // PAIR
+    z_count = lax.axis_size("dp")
+    cap = PAIR * CAP
+    tok_count, width = tokens.shape
+    hidden = gate_weight.shape[2]
+    count = PAIR * y_count * z_count * cap
+    dma = pltpu.SemaphoreType.DMA
+    rows, dcat, grad = pl.pallas_call(
+        functools.partial(move_kernel, (y_count, z_count, cap)),
+        out_shape=(
+            jax.ShapeDtypeStruct((count, width + 128), jnp.bfloat16),
+            jax.ShapeDtypeStruct((count, 2 * hidden), jnp.bfloat16),
+            jax.ShapeDtypeStruct(route_ids.shape[::-1], jnp.float32),
+        ),
+        in_specs=[pl.BlockSpec(memory_space=pltpu.VMEM)] * 2 + [pl.BlockSpec(memory_space=pl.ANY)] * 5,
+        out_specs=[pl.BlockSpec(memory_space=pltpu.VMEM)] * 3,
+        scratch_shapes=[
+            pltpu.VMEM((count, width), jnp.bfloat16),
+            pltpu.VMEM((tok_count, width), jnp.bfloat16),
+            pltpu.VMEM((tok_count, width), jnp.bfloat16),
+            pltpu.VMEM((width, hidden), jnp.bfloat16),
+            pltpu.VMEM((width, hidden), jnp.bfloat16),
+            pltpu.VMEM((hidden, width), jnp.bfloat16),
+            pltpu.VMEM((y_count * cap, width + 128), jnp.bfloat16),
+            pltpu.VMEM((y_count * cap, width), jnp.bfloat16),
+            pltpu.VMEM((count, 128), jnp.float32),
+            pltpu.VMEM((count, 128), jnp.float32),
+            dma((5,)),
+            dma((y_count, 2)),
+            dma((z_count, y_count, 2)),
+            dma((z_count, y_count, 2)),
+            dma((z_count, y_count, 2)),
+            dma((z_count, PAIR, y_count, 2)),
+            dma((z_count, PAIR, y_count)),
+            dma((PAIR * y_count * z_count,)),
+        ],
+        compiler_params=pltpu.CompilerParams(
+            collective_id=0, has_side_effects=True, vmem_limit_bytes=48 * 2**20
+        ),
+        cost_estimate=pl.CostEstimate(
+            flops=6 * count * width * hidden, bytes_accessed=8 * width * hidden, transcendentals=count * hidden
+        ),
+    )(route_ids.T, route_weight.T, tokens, cotangent, gate_weight[0], up_weight[0], down_weight[0])
+    row_block = rows[:, :width]
+    grad_gate = dot_first(row_block, dcat[:, :hidden]).astype(jnp.bfloat16)
+    grad_up = dot_first(row_block, dcat[:, hidden:]).astype(jnp.bfloat16)
+    return grad_gate[None], grad_up[None], grad.T
+
+
+def fits(mesh):
+    return mesh.shape["expert"] % PAIR == 0 and mesh.shape["expert"] * mesh.shape["dp"] <= 16
+
+
 def solution(mesh):
     return jax.shard_map(
-        general,
+        moved if fits(mesh) else general,
         mesh=mesh,
         in_specs=(
             P(("groups", "expert", "dp"), None),

time: 139 us -> 93.2 us (0.67)
  waiting for transfers between devices: 86.1 us -> 0 us
  Pallas kernels: 0 us -> 79.1 us
  starting transfers between devices: 15.3 us -> 0 us
  matrix products: 21.1 us -> 8.21 us
  blocking collectives: 8.93 us -> 0 us
  other arithmetic: 1.67 us -> 0 us
    all_to_all x3 -> x0, waiting for transfers between devices: 86.1 us -> none  [exchange(): lax.all_to_all(array, ('expert', 'dp'), split_axis=0, concat_axis=0, tile...]
    pallas_call x0 -> x1, Pallas kernels: none -> 79.1 us  [moved(): pl.pallas_call(functools.partial(move_kernel, (y_count, z_count, cap)), o...]
    all_to_all x3 -> x0, starting transfers between devices: 15.3 us -> none  [exchange(): lax.all_to_all(array, ('expert', 'dp'), split_axis=0, concat_axis=0, tile...]
    dot_general x4 -> x0, matrix products: 9.72 us -> none  [the longest x1 4.02 us: general(): lax.dot_general(cot_block, down_weight[0], (((1,), (1,)), ((), ())), pref...]
    all_to_all x1 -> x0, blocking collectives: 8.93 us -> none  [exchange(): lax.all_to_all(array, ('expert', 'dp'), split_axis=0, concat_axis=0, tile...]
    unnamed x8 -> x11, local copies, waits for them, and re-layouts: 0.73 us -> 4.96 us
    dot_general x4 -> x2, matrix products: 11.4 us -> 8.21 us  [dot_first(): lax.dot_general(a, b, (((0,), (0,)), ((), ())), preferred_element_type=jn...]
    broadcast_in_dim x3 -> x0, local copies, waits for them, and re-layouts: 2.83 us -> none  [widen_rows(): jnp.broadcast_to(array[:, None], (expert_count, dp_count) + array.shape[1:])]
  transfers between devices with their start and end apart: 3 -> 0, of which waited for: 3 -> 0; matrix products, arithmetic and copies ran while one was open for 5% -> 0% of each run, Pallas kernels for 0% -> 0%
where the time goes in v2:
time: 93.2 us; the launch traced here: 93 us
  Pallas kernels  79.1 us (85%)
  matrix products  8.21 us (9%)
  local copies, waits for them, and re-layouts  4.96 us (5%)
    pallas_call x1, Pallas kernels, moved(): pl.pallas_call(functools.partial(move_kernel, (y_count, z_count, cap)), o...  79.1 us
    dot_general x2, matrix products, dot_first(): lax.dot_general(a, b, (((0,), (0,)), ((), ())), preferred_element_type=jn...  8.21 us
    unnamed x11, local copies, waits for them, and re-layouts  4.96 us

profile of v2, /device:TPU:0, one launch (start us, length us, event | category | flops | bytes accessed | tf_op | source)
XLA Modules:
  0.0 93.0 jit_solution(5991020443513676896)
XLA Ops:
  0.6 0.0 copy-start
  0.6 1.5 %copy-done = bf16[128,7168]{1,0:T(8,128)(2,1)S(1)} copy-done((bf16[128,7168]{1,0:T(8,128)(2,1)S(1)}, bf16[128,7168]{1,0:T(8,128)(2,1)}, u32[]{:S(2)}) %copy-start) | copy-done | bytes 1835032
  2.1 0.0 copy-start.1
  2.1 1.5 %copy-done.1 = bf16[128,7168]{1,0:T(8,128)(2,1)S(1)} copy-done((bf16[128,7168]{1,0:T(8,128)(2,1)S(1)}, bf16[128,7168]{1,0:T(8,128)(2,1)}, u32[]{:S(2)}) %copy-start.1) | copy-done | bytes 1835032
  3.6 0.0 copy-start.2
  3.6 0.7 copy-done.2
  4.3 0.0 copy-start.3
  4.3 0.7 copy-done.3
  5.0 79.1 %shard_map.94 = (bf16[256,7296]{1,0:T(8,128)(2,1)}, bf16[256,512]{1,0:T(8,128)(2,1)S(1)}, f32[8,128]{1,0:T(8,128)S(1)}) custom-call(s32[8,128]{1,0:T(8,128)S(1)} %bitcast.10, bf16[8,128]{1,0:T(8,128)(2,1)S(1)} %bitcast.12, bf16[128,7168]{1,0:T(8,128)(2,1)S(1)} %copy-done, bf16[128,7168]{1,0:T(8,128)(2,1)S(1)} %copy-done.1, bf16[7168,256]{1,0:T(8,128)(2,1)} %bitcast.13, ...), custom_call_target="tpu_custom_call" | custom-call | flops 2818572288 | bytes 14680064 | tf_op jit(solution)/shard_map/pallas_call | solution.py:368
  84.1 0.0 copy-start.4
  84.2 5.2 %fusion.1 = bf16[1,7168,256]{2,1,0:T(8,128)(2,1)} fusion(bf16[256,7296]{1,0:T(8,128)(2,1)} %get-tuple-element.6, bf16[256,512]{1,0:T(8,128)(2,1)S(1)} %get-tuple-element.7), kind=kOutput, calls=%fused_computation.3 | convolution fusion | flops 941359104 | bytes 7471104 | tf_op jit(solution)/shard_map/dot_general | solution.py:15
  89.4 0.0 copy-done.4
  89.4 3.0 %fusion = bf16[1,7168,256]{2,1,0:T(8,128)(2,1)} fusion(bf16[256,7296]{1,0:T(8,128)(2,1)S(1)} %copy-done.4, bf16[256,512]{1,0:T(8,128)(2,1)S(1)} %get-tuple-element.7), kind=kOutput, calls=%fused_computation.2 | convolution fusion | flops 941359104 | bytes 7471104 | tf_op jit(solution)/shard_map/dot_general | solution.py:15
  92.4 0.6 copy.11
Async XLA Ops:
  0.6 1.5 %copy-start = (bf16[128,7168]{1,0:T(8,128)(2,1)S(1)}, bf16[128,7168]{1,0:T(8,128)(2,1)}, u32[]{:S(2)}) copy-start(bf16[128,7168]{1,0:T(8,128)(2,1)} %tok_hbm.1) | copy-start | bytes 5505028
  2.1 1.5 %copy-start.1 = (bf16[128,7168]{1,0:T(8,128)(2,1)S(1)}, bf16[128,7168]{1,0:T(8,128)(2,1)}, u32[]{:S(2)}) copy-start(bf16[128,7168]{1,0:T(8,128)(2,1)} %cot_hbm.1) | copy-start | bytes 5505028
  3.6 0.7 copy-start.2
  4.3 0.7 copy-start.3
  84.1 5.2 %copy-start.4 = (bf16[256,7296]{1,0:T(8,128)(2,1)S(1)}, bf16[256,7296]{1,0:T(8,128)(2,1)}, u32[]{:S(2)}) copy-start(bf16[256,7296]{1,0:T(8,128)(2,1)} %get-tuple-element.6) | copy-start | bytes 11206660

commit v3 on v1

--- a/solution.py
+++ b/solution.py
@@ -1,6 +1,11 @@
+import functools
+import math
+
 import jax
 import jax.numpy as jnp
 from jax import lax
+from jax.experimental import pallas as pl
+from jax.experimental.pallas import tpu as pltpu
 from jax.sharding import PartitionSpec as P
 
 CAP = 8
@@ -58,9 +63,386 @@
     return grad_gate[None], grad_up[None], route_grad
 
 
+PAIR = 2
+UNIT = 3 * CAP
+PIECES = 4
+
+
+def move_kernel(
+    z_count, ids_hbm, rw_hbm, tok_hbm, cot_hbm, wg_hbm, wu_hbm, wd_hbm,
+    rows_ref, dcat_ref, grad_ref, flag_ref,
+    ids_ref, rw_ref, tok_ref, cot_ref, wg_ref, wu_ref, wd_ref, send_ref, got_ref, pbuf, rbuf,
+    load_sem, y_send, y_recv, up_sem, down_sem, core_sem, recv_sem, back_sem, home_sem,
+):
+    y_count = 2
+    toks, width = tok_ref.shape
+    hidden = wg_ref.shape[1]
+    piece = width // PIECES
+    both = 2 * UNIT
+    message = UNIT + 8
+    experts = PAIR * y_count
+    group = experts * z_count
+    me = lax.axis_index("expert")
+    z = lax.axis_index("dp")
+    y, c = lax.div(me, PAIR), lax.rem(me, PAIR)
+    mine = me * z_count + z
+
+    loads = [
+        pltpu.make_async_copy(src, dst, load_sem.at[i])
+        for i, (src, dst) in enumerate(
+            (
+                (ids_hbm, ids_ref), (rw_hbm, rw_ref), (tok_hbm, tok_ref), (cot_hbm, cot_ref),
+                (wg_hbm, wg_ref), (wu_hbm, wu_ref), (wd_hbm, wd_ref),
+            )
+        )
+    ]
+    for load in loads:
+        load.start()
+
+    barrier = pltpu.get_barrier_semaphore()
+    for step in range(1, group):
+        other = lax.rem(mine + step, group)
+        pl.semaphore_signal(
+            barrier, inc=1, device_id={"expert": lax.div(other, z_count), "dp": lax.rem(other, z_count)},
+            device_id_type=pl.DeviceIdType.MESH,
+        )
+
+    loads[0].wait()
+    loads[1].wait()
+    ids = ids_ref[...]
+    rw = rw_ref[...].astype(jnp.float32)
+    padded = -(-experts // 16) * 16
+    number = lax.broadcasted_iota(jnp.int32, (padded, toks), 0)
+    chosen = jnp.zeros((padded, toks), jnp.float32)
+    for k in range(ids.shape[0]):
+        chosen += jnp.where(ids[k : k + 1, :] == number, 1.0, 0.0)
+    earlier = lax.broadcasted_iota(jnp.int32, (toks, toks), 0) < lax.broadcasted_iota(jnp.int32, (toks, toks), 1)
+    upper = jnp.where(earlier, 1.0, 0.0).astype(jnp.bfloat16)
+    rank = jnp.dot(chosen.astype(jnp.bfloat16), upper, preferred_element_type=jnp.float32)
+    total = jnp.sum(chosen, axis=1, keepdims=True)
+    slot = lax.broadcasted_iota(jnp.int32, (both, toks), 0).astype(jnp.float32)
+    lane = lax.broadcasted_iota(jnp.int32, (both, 128), 1)
+    select = jnp.zeros((both, toks), jnp.float32)
+    tail = jnp.zeros((both, 128), jnp.float32)
+    most = jnp.zeros((1, 1), jnp.float32)
+    picks = []
+    for e in range(experts):
+        here = jnp.where(y == e // PAIR, 1.0, 0.0)
+        spot = rank[e : e + 1, :]
+        if e % PAIR:
+            spot = spot + total[e - 1 : e, :]
+            most = jnp.maximum(most, total[e - 1 : e, :] + total[e : e + 1, :])
+        spot = here * spot + (1.0 - here) * (both - 1.0 - spot)
+        pick = jnp.where((slot == spot) & (chosen[e : e + 1, :] > 0.5), 1.0, 0.0)
+        weight = jnp.sum(jnp.where(ids == e, rw, 0.0), axis=0, keepdims=True)
+        tail += jnp.where(lane == e % PAIR, jnp.sum(pick * weight, axis=1, keepdims=True), 0.0)
+        select += pick
+        picks.append(pick[:UNIT] + pick[UNIT:])
+    select = select.astype(jnp.bfloat16)
+    over = jnp.broadcast_to(jnp.where(most > UNIT // 2 + 0.5, 1.0, 0.0), (8, 128))
+
+    def unit(z_src, c_src):
+        return pl.multiple_of((z_src * PAIR + c_src) * both, 16)
+
+    def columns(p):
+        return pl.ds(p * piece, piece + (128 if p == PIECES - 1 else 0))
+
+    def remote(src, dst, send, recv, target):
+        return pltpu.make_async_remote_copy(
+            src_ref=src, dst_ref=dst, send_sem=send, recv_sem=recv, device_id=target,
+            device_id_type=pl.DeviceIdType.MESH,
+        )
+
+    def relay(z_src, p, send, target, c_src=c):
+        there = rows_ref.at[pl.ds(unit(z_src, c_src), both), columns(p)]
+        return remote(there, there, send, recv_sem.at[z_src, c_src, p], target)
+
+    def to_up(z_src, p):
+        return relay(z_src, p, up_sem.at[z_src, p], {"dp": z + 1})
+
+    def to_down(z_src, p):
+        return relay(z_src, p, down_sem.at[z_src, p], {"dp": z - 1})
+
+    def to_core(z_src, p):
+        return relay(z_src, p, core_sem.at[z_src, p], {"expert": y * PAIR + 1 - c})
+
+    def arrived(z_src, c_src, p):
+        relay(z_src, p, load_sem.at[0], {"expert": y * PAIR + 1 - c}, c_src).wait_recv()
+
+    def across(p):
+        return remote(
+            send_ref.at[:, columns(p)], got_ref.at[:, columns(p)], y_send.at[p], y_recv.at[p],
+            {"expert": (1 - y) * PAIR + c},
+        )
+
+    own = pl.ds(unit(z, c), both)
+    loads[2].wait()
+    loads[3].wait()
+    for p in range(PIECES):
+        at = pl.ds(p * piece, piece)
+        x = jnp.dot(select, tok_ref[:, at], preferred_element_type=jnp.float32)
+        t = jnp.dot(select, cot_ref[:, at], preferred_element_type=jnp.float32)
+        rows_ref[own, at] = jnp.concatenate([x[:UNIT], t[:UNIT]], axis=0).astype(jnp.bfloat16)
+        send_ref[:, at] = jnp.concatenate([x[UNIT:], t[UNIT:]], axis=0).astype(jnp.bfloat16)
+        if p == PIECES - 1:
+            blank = jnp.zeros((UNIT, 128), jnp.float32)
+            rows_ref[own, width:] = jnp.concatenate([tail[:UNIT], blank], axis=0).astype(jnp.bfloat16)
+            send_ref[:, width:] = jnp.concatenate([tail[UNIT:], blank], axis=0).astype(jnp.bfloat16)
+        if p == 0:
+            pl.semaphore_wait(barrier, group - 1)
+        across(p).start()
+    for p in range(PIECES):
+        across(p).wait_recv()
+        rows_ref[own, columns(p)] = rows_ref[own, columns(p)] + got_ref[:, columns(p)]
+
+        @pl.when(z + 1 < z_count)
+        def _(p=p):
+            to_up(z, p).start()
+
+        @pl.when(z > 0)
+        def _(p=p):
+            to_down(z, p).start()
+
+        to_core(z, p).start()
+
+    plane = PAIR * both
+
+    def forward(z_src):
+        for p in range(PIECES):
+            arrived(z_src, 1 - c, p)
+        first = pl.multiple_of(z_src * plane, 16)
+        rows = pl.ds(first, plane)
+
+        def add(i, sums):
+            at = pl.ds(pl.multiple_of(i * piece, 128), piece)
+            x = rows_ref[rows, at]
+            return (
+                sums[0] + jnp.dot(x, wg_ref[at, :], preferred_element_type=jnp.float32),
+                sums[1] + jnp.dot(x, wu_ref[at, :], preferred_element_type=jnp.float32),
+                sums[2]
+                + lax.dot_general(x, wd_ref[:, at], (((1,), (1,)), ((), ())), preferred_element_type=jnp.float32),
+            )
+
+        zero = jnp.zeros((plane, hidden), jnp.float32)
+        gates, ups, backs = lax.fori_loop(0, PIECES, add, (zero, zero, zero))
+        marks = rows_ref[rows, width:].astype(jnp.float32)
+        which = lax.broadcasted_iota(jnp.int32, (UNIT, 128), 1)
+        blank = jnp.zeros((UNIT, hidden), jnp.float32)
+        for k in range(PAIR):
+            low, high = k * both, k * both + UNIT
+            gate_pre, up_pre, back = gates[low:high], ups[low:high], backs[high : high + UNIT]
+            sig = jax.nn.sigmoid(gate_pre)
+            act = gate_pre * sig
+            part = jnp.sum(act * up_pre * back, axis=1, keepdims=True)
+            start = pl.multiple_of((z_src * PAIR + k) * message, 8)
+            pbuf[pl.ds(start, UNIT), :] = jnp.broadcast_to(part, (UNIT, 128))
+            pbuf[pl.ds(start + UNIT, 8), :] = over
+            weight = jnp.sum(jnp.where(which == c, marks[low:high], 0.0), axis=1, keepdims=True)
+            act_grad = weight * back
+            d_gate = act_grad * up_pre * sig * (1.0 + gate_pre * (1.0 - sig))
+            d_up = act_grad * act
+            out = pl.ds(pl.multiple_of(first + k * both, 16), both)
+            dcat_ref[out, :hidden] = jnp.concatenate([d_gate, blank], axis=0).astype(jnp.bfloat16)
+            dcat_ref[out, hidden:] = jnp.concatenate([d_up, blank], axis=0).astype(jnp.bfloat16)
+
+    def sums_of(z_to, c_to):
+        return pbuf.at[pl.ds(pl.multiple_of((z_to * PAIR + c_to) * message, 8), message), :]
+
+    def sums_from(index):
+        return rbuf.at[pl.ds(pl.multiple_of(index * message, 8), message), :]
+
+    def home(z_to, c_to, y_to):
+        return remote(
+            sums_of(z_to, c_to), sums_from(mine), back_sem.at[z_to, c_to, y_to], home_sem.at[mine],
+            {"expert": y_to * PAIR + c_to, "dp": z_to},
+        )
+
+    def not_me(z_to, c_to, y_to):
+        return (z_to != z) | (c_to != c) | (y_to != y)
+
+    def finish(z_src):
+        forward(z_src)
+        for c_to in range(PAIR):
+            for y_to in range(y_count):
+
+                @pl.when(not_me(z_src, c_to, y_to))
+                def _(c_to=c_to, y_to=y_to):
+                    home(z_src, c_to, y_to).start()
+
+    def finish_hop(hop):
+        if hop == 0:
+            finish(z)
+            return
+
+        @pl.when(z >= hop)
+        def _():
+            finish(z - hop)
+
+        @pl.when(z + hop < z_count)
+        def _():
+            finish(z + hop)
+
+    for load in loads[4:]:
+        load.wait()
+    for hop in range(1, z_count):
+        for p in range(PIECES):
+
+            @pl.when(z >= hop)
+            def _(p=p, hop=hop):
+                arrived(z - hop, c, p)
+
+                @pl.when(z + 1 < z_count)
+                def _():
+                    to_up(z - hop, p).start()
+
+                to_core(z - hop, p).start()
+
+            @pl.when(z + hop < z_count)
+            def _(p=p, hop=hop):
+                arrived(z + hop, c, p)
+
+                @pl.when(z > 0)
+                def _():
+                    to_down(z + hop, p).start()
+
+                to_core(z + hop, p).start()
+
+            if p == 1:
+                finish_hop(hop - 1)
+    finish_hop(z_count - 1)
+
+    rbuf[pl.ds(pl.multiple_of(mine * message, 8), message), :] = pbuf[
+        pl.ds(pl.multiple_of((z * PAIR + c) * message, 8), message), :
+    ]
+
+    for p in range(PIECES):
+        across(p).wait_send()
+        for z_src in range(z_count):
+            to_core(z_src, p).wait_send()
+
+            @pl.when((z_src <= z) & (z + 1 < z_count))
+            def _(p=p, z_src=z_src):
+                to_up(z_src, p).wait_send()
+
+            @pl.when((z_src >= z) & (z > 0))
+            def _(p=p, z_src=z_src):
+                to_down(z_src, p).wait_send()
+
+    for z_to in range(z_count):
+        for c_to in range(PAIR):
+            for y_to in range(y_count):
+
+                @pl.when(not_me(z_to, c_to, y_to))
+                def _(z_to=z_to, c_to=c_to, y_to=y_to):
+                    home(z_to, c_to, y_to).wait_send()
+                    index = (y_to * PAIR + c_to) * z_count + z_to
+                    remote(
+                        sums_from(index), sums_from(index), load_sem.at[0], home_sem.at[index],
+                        {"expert": y * PAIR + 1 - c},
+                    ).wait_recv()
+
+    result = jnp.zeros(ids.shape, jnp.float32)
+    flags = over
+    for e in range(experts):
+        sums = jnp.zeros((UNIT, 128), jnp.float32)
+        for k in range(z_count):
+            first = (e * z_count + k) * message
+            sums = sums + rbuf[first : first + UNIT, :]
+            flags = jnp.maximum(flags, rbuf[first + UNIT : first + message, :])
+        value = jnp.sum(picks[e] * sums, axis=0, keepdims=True)
+        result += jnp.where(ids == e, value, 0.0)
+    grad_ref[...] = result
+    flag_ref[...] = flags
+
+
+def back_kernel(rows_ref, dcat_ref, gate_ref, up_ref):
+    hidden = gate_ref.shape[1]
+    both = dot_first(rows_ref[...], dcat_ref[...]).astype(jnp.bfloat16)
+    gate_ref[...] = both[:, :hidden]
+    up_ref[...] = both[:, hidden:]
+
+
+def moved(*args):
+    tokens, cotangent, route_ids, route_weight, gate_weight, up_weight, down_weight = args
+    y_count = lax.axis_size("expert") // PAIR
+    z_count = lax.axis_size("dp")
+    tok_count, width = tokens.shape
+    hidden = gate_weight.shape[2]
+    both = 2 * UNIT
+    units = PAIR * z_count
+    group = units * y_count
+    message = UNIT + 8
+    dma = pltpu.SemaphoreType.DMA
+    rows, dcat, grad, flag = pl.pallas_call(
+        functools.partial(move_kernel, z_count),
+        out_shape=(
+            jax.ShapeDtypeStruct((units * both, width + 128), jnp.bfloat16),
+            jax.ShapeDtypeStruct((units * both, 2 * hidden), jnp.bfloat16),
+            jax.ShapeDtypeStruct(route_ids.shape[::-1], jnp.float32),
+            jax.ShapeDtypeStruct((8, 128), jnp.float32),
+        ),
+        in_specs=[pl.BlockSpec(memory_space=pl.ANY)] * 7,
+        out_specs=[pl.BlockSpec(memory_space=pltpu.VMEM)] * 4,
+        scratch_shapes=[
+            pltpu.VMEM(route_ids.shape[::-1], jnp.int32),
+            pltpu.VMEM(route_ids.shape[::-1], jnp.float32),
+            pltpu.VMEM((tok_count, width), jnp.bfloat16),
+            pltpu.VMEM((tok_count, width), jnp.bfloat16),
+            pltpu.VMEM((width, hidden), jnp.bfloat16),
+            pltpu.VMEM((width, hidden), jnp.bfloat16),
+            pltpu.VMEM((hidden, width), jnp.bfloat16),
+            pltpu.VMEM((both, width + 128), jnp.bfloat16),
+            pltpu.VMEM((both, width + 128), jnp.bfloat16),
+            pltpu.VMEM((units * message, 128), jnp.float32),
+            pltpu.VMEM((group * message, 128), jnp.float32),
+            dma((7,)),
+            dma((PIECES,)),
+            dma((PIECES,)),
+            dma((z_count, PIECES)),
+            dma((z_count, PIECES)),
+            dma((z_count, PIECES)),
+            dma((z_count, PAIR, PIECES)),
+            dma((z_count, PAIR, y_count)),
+            dma((group,)),
+        ],
+        compiler_params=pltpu.CompilerParams(
+            collective_id=0, has_side_effects=True, vmem_limit_bytes=60 * 2**20
+        ),
+        cost_estimate=pl.CostEstimate(
+            flops=6 * units * both * width * hidden,
+            bytes_accessed=8 * width * hidden,
+            transcendentals=units * UNIT * hidden,
+        ),
+    )(
+        route_ids.T, route_weight.T.astype(jnp.float32), tokens, cotangent,
+        gate_weight[0], up_weight[0], down_weight[0],
+    )
+
+    def fitting():
+        tile = math.gcd(width, 1024)
+        gate, up = pl.pallas_call(
+            back_kernel,
+            out_shape=(jax.ShapeDtypeStruct((width, hidden), jnp.bfloat16),) * 2,
+            grid=(width // tile,),
+            in_specs=[
+                pl.BlockSpec((units * both, tile), lambda i: (0, i)),
+                pl.BlockSpec((units * both, 2 * hidden), lambda i: (0, 0)),
+            ],
+            out_specs=(pl.BlockSpec((tile, hidden), lambda i: (i, 0)),) * 2,
+            compiler_params=pltpu.CompilerParams(vmem_limit_bytes=60 * 2**20),
+        )(rows, dcat)
+        return gate[None], up[None], grad.T
+
+    return lax.cond(flag[0, 0] > 0.5, lambda: general(*args), fitting)
+
+
+def fits(mesh):
+    return mesh.shape["expert"] == 2 * PAIR and mesh.shape["dp"] <= 8
+
+
 def solution(mesh):
     return jax.shard_map(
-        general,
+        moved if fits(mesh) else general,
         mesh=mesh,
         in_specs=(
             P(("groups", "expert", "dp"), None),

time: 139 us -> 87.2 us (0.63)
  waiting for transfers between devices: 86.1 us -> 0 us
  Pallas kernels: 0 us -> 81.7 us
  matrix products: 21.1 us -> 0 us
  starting transfers between devices: 15.3 us -> 0 us
  blocking collectives: 8.93 us -> 0 us
  local copies, waits for them, and re-layouts: 4.44 us -> 2.47 us
    all_to_all x3 -> x0, waiting for transfers between devices: 86.1 us -> none  [exchange(): lax.all_to_all(array, ('expert', 'dp'), split_axis=0, concat_axis=0, tile...]
    pallas_call x0 -> x2, Pallas kernels: none -> 81.7 us  [the longest x1 72 us: moved(): pl.pallas_call(functools.partial(move_kernel, z_count), out_shape=(jax.Sh...]
    dot_general x8 -> x0, matrix products: 21.1 us -> none  [the longest x4 11.4 us: dot_first(): lax.dot_general(a, b, (((0,), (0,)), ((), ())), preferred_element_type=jn...]
    all_to_all x3 -> x0, starting transfers between devices: 15.3 us -> none  [exchange(): lax.all_to_all(array, ('expert', 'dp'), split_axis=0, concat_axis=0, tile...]
    all_to_all x1 -> x0, blocking collectives: 8.93 us -> none  [exchange(): lax.all_to_all(array, ('expert', 'dp'), split_axis=0, concat_axis=0, tile...]
    broadcast_in_dim x3 -> x0, local copies, waits for them, and re-layouts: 2.83 us -> none  [widen_rows(): jnp.broadcast_to(array[:, None], (expert_count, dp_count) + array.shape[1:])]
  transfers between devices with their start and end apart: 3 -> 0, of which waited for: 3 -> 0; matrix products, arithmetic and copies ran while one was open for 5% -> 0% of each run, Pallas kernels for 0% -> 0%
where the time goes in v3:
time: 87.2 us; the launch traced here: 86.8 us
  Pallas kernels  81.7 us (94%)
  local copies, waits for them, and re-layouts  2.47 us (3%)
  between operations  1.3 us (1%)
  other arithmetic  1.28 us (1%)
    pallas_call x1, Pallas kernels, moved(): pl.pallas_call(functools.partial(move_kernel, z_count), out_shape=(jax.Sh...  72 us
    pallas_call x1, Pallas kernels, fitting(): pl.pallas_call(back_kernel, out_shape=(jax.ShapeDtypeStruct((width, hidde...  9.7 us

profile of v3, /device:TPU:0, one launch (start us, length us, event | category | flops | bytes accessed | tf_op | source)
XLA Modules:
  0.0 86.8 jit_solution(8290718743882294844)
XLA Ops:
  0.6 1.3 %convert_bitcast_fusion.rw_hbm = f32[8,128]{1,0:T(8,128)} fusion(bf16[128,8]{0,1:T(8,128)(2,1)} %param.12), kind=kLoop, calls=%fused_computation.46 | loop fusion | flops 1024 | bytes 6144 | tf_op jit(solution)/shard_map/convert_element_type | solution.py:417
  1.9 0.0 copy-start.1
  1.9 0.0 copy-start.2
  1.9 0.0 copy-start.3
  1.9 72.0 %shard_map.94 = (bf16[384,7296]{1,0:T(8,128)(2,1)}, bf16[384,512]{1,0:T(8,128)(2,1)S(1)}, f32[8,128]{1,0:T(8,128)}, f32[8,128]{1,0:T(8,128)}) custom-call(s32[8,128]{1,0:T(8,128)} %bitcast.64, f32[8,128]{1,0:T(8,128)} %convert_bitcast_fusion.rw_hbm, bf16[128,7168]{1,0:T(8,128)(2,1)} %tok_hbm.1, bf16[128,7168]{1,0:T(8,128)(2,1)} %cot_hbm.1, ...), custom_call_target="tpu_custom_call" | custom-call | flops 4227858432 | bytes 14680064 | tf_op jit(solution)/shard_map/pallas_call | solution.py:376
  73.9 1.2 %slice.3 = f32[1,1]{1,0:T(1,128)} slice(f32[8,128]{1,0:T(8,128)} %get-tuple-element.39), slice={[0:1], [0:1]} | slice | bytes 8 | tf_op jit(solution)/shard_map/slice | solution.py:436
  75.8 0.7 copy.35
  76.4 0.0 copy-done.1
  76.4 0.0 copy-done.2
  76.5 0.0 copy-done.3
  76.5 9.7 %conditional.1 = (f32[128,8]{0,1:T(8,128)S(1)}, bf16[7168,256]{1,0:T(8,128)(2,1)}, bf16[7168,256]{1,0:T(8,128)(2,1)}) conditional(s32[]{:T(128)} %bitcast.20, (bf16[384,7296]{1,0:T(8,128)(2,1)}, bf16[384,512]{1,0:T(8,128)(2,1)S(1)}, f32[8,128]{1,0:T(8,128)S(1)}) %tuple.31, (s32[128,8]{0,1:T(8,128)S(1)}, bf16[128,7168]{1,0:T(8,128)(2,1)S(1)}, ...), branch_computations={%region_0.0_spmd, %region_1.9_spmd} | conditional | flops 2471422976 | bytes 63769240 | solution.py:436
  76.5 9.7 %branch_0_fun.1 = (bf16[7168,256]{1,0:T(8,128)(2,1)}, bf16[7168,256]{1,0:T(8,128)(2,1)}) custom-call(bf16[384,7296]{1,0:T(8,128)(2,1)} %get-tuple-element.20.rows_ref, bf16[384,512]{1,0:T(8,128)(2,1)S(1)} %get-tuple-element.21.dcat_ref), custom_call_target="tpu_custom_call" | custom-call | tf_op jit(solution)/shard_map/cond/branch_0_fun/pallas_call | solution.py:423
  86.2 0.0 copy-start.4
  86.2 0.6 copy-done.4
Async XLA Ops:
  1.9 74.5 %copy-start.1 = (bf16[128,7168]{1,0:T(8,128)(2,1)S(1)}, bf16[128,7168]{1,0:T(8,128)(2,1)}, u32[]{:S(2)}) copy-start(bf16[128,7168]{1,0:T(8,128)(2,1)} %tok_hbm.1) | copy-start | bytes 5505028
  1.9 74.5 %copy-start.2 = (s32[128,8]{0,1:T(8,128)S(1)}, s32[128,8]{0,1:T(8,128)}, u32[]{:S(2)}) copy-start(s32[128,8]{0,1:T(8,128)} %param.11) | copy-start | bytes 12292
  1.9 74.5 %copy-start.3 = (bf16[128,8]{0,1:T(8,128)(2,1)S(1)}, bf16[128,8]{0,1:T(8,128)(2,1)}, u32[]{:S(2)}) copy-start(bf16[128,8]{0,1:T(8,128)(2,1)} %param.12) | copy-start | bytes 6148
  86.2 0.6 copy-start.4

commit v4 on v3

--- a/solution.py
+++ b/solution.py
@@ -70,8 +70,8 @@
 
 def move_kernel(
     z_count, ids_hbm, rw_hbm, tok_hbm, cot_hbm, wg_hbm, wu_hbm, wd_hbm,
-    rows_ref, dcat_ref, grad_ref, flag_ref,
-    ids_ref, rw_ref, tok_ref, cot_ref, wg_ref, wu_ref, wd_ref, send_ref, got_ref, pbuf, rbuf,
+    kept_ref, dcat_ref, grad_ref, flag_ref,
+    rows_ref, ids_ref, rw_ref, tok_ref, cot_ref, wg_ref, wu_ref, wd_ref, send_ref, got_ref, pbuf, rbuf,
     load_sem, y_send, y_recv, up_sem, down_sem, core_sem, recv_sem, back_sem, home_sem,
 ):
     y_count = 2
@@ -216,6 +216,9 @@
         def add(i, sums):
             at = pl.ds(pl.multiple_of(i * piece, 128), piece)
             x = rows_ref[rows, at]
+            kept_ref[pl.ds(pl.multiple_of(z_src * both, 16), both), at] = jnp.concatenate(
+                [x[:UNIT], x[both : both + UNIT]], axis=0
+            )
             return (
                 sums[0] + jnp.dot(x, wg_ref[at, :], preferred_element_type=jnp.float32),
                 sums[1] + jnp.dot(x, wu_ref[at, :], preferred_element_type=jnp.float32),
@@ -227,7 +230,7 @@
         gates, ups, backs = lax.fori_loop(0, PIECES, add, (zero, zero, zero))
         marks = rows_ref[rows, width:].astype(jnp.float32)
         which = lax.broadcasted_iota(jnp.int32, (UNIT, 128), 1)
-        blank = jnp.zeros((UNIT, hidden), jnp.float32)
+        gate_parts, up_parts = [], []
         for k in range(PAIR):
             low, high = k * both, k * both + UNIT
             gate_pre, up_pre, back = gates[low:high], ups[low:high], backs[high : high + UNIT]
@@ -241,9 +244,11 @@
             act_grad = weight * back
             d_gate = act_grad * up_pre * sig * (1.0 + gate_pre * (1.0 - sig))
             d_up = act_grad * act
-            out = pl.ds(pl.multiple_of(first + k * both, 16), both)
-            dcat_ref[out, :hidden] = jnp.concatenate([d_gate, blank], axis=0).astype(jnp.bfloat16)
-            dcat_ref[out, hidden:] = jnp.concatenate([d_up, blank], axis=0).astype(jnp.bfloat16)
+            gate_parts.append(d_gate)
+            up_parts.append(d_up)
+        out = pl.ds(pl.multiple_of(z_src * both, 16), both)
+        dcat_ref[out, :hidden] = jnp.concatenate(gate_parts, axis=0).astype(jnp.bfloat16)
+        dcat_ref[out, hidden:] = jnp.concatenate(up_parts, axis=0).astype(jnp.bfloat16)
 
     def sums_of(z_to, c_to):
         return pbuf.at[pl.ds(pl.multiple_of((z_to * PAIR + c_to) * message, 8), message), :]
@@ -376,14 +381,15 @@
     rows, dcat, grad, flag = pl.pallas_call(
         functools.partial(move_kernel, z_count),
         out_shape=(
-            jax.ShapeDtypeStruct((units * both, width + 128), jnp.bfloat16),
-            jax.ShapeDtypeStruct((units * both, 2 * hidden), jnp.bfloat16),
+            jax.ShapeDtypeStruct((units * UNIT, width), jnp.bfloat16),
+            jax.ShapeDtypeStruct((units * UNIT, 2 * hidden), jnp.bfloat16),
             jax.ShapeDtypeStruct(route_ids.shape[::-1], jnp.float32),
             jax.ShapeDtypeStruct((8, 128), jnp.float32),
         ),
         in_specs=[pl.BlockSpec(memory_space=pl.ANY)] * 7,
         out_specs=[pl.BlockSpec(memory_space=pltpu.VMEM)] * 4,
         scratch_shapes=[
+            pltpu.VMEM((units * both, width + 128), jnp.bfloat16),
             pltpu.VMEM(route_ids.shape[::-1], jnp.int32),
             pltpu.VMEM(route_ids.shape[::-1], jnp.float32),
             pltpu.VMEM((tok_count, width), jnp.bfloat16),
@@ -425,8 +431,8 @@
             out_shape=(jax.ShapeDtypeStruct((width, hidden), jnp.bfloat16),) * 2,
             grid=(width // tile,),
             in_specs=[
-                pl.BlockSpec((units * both, tile), lambda i: (0, i)),
-                pl.BlockSpec((units * both, 2 * hidden), lambda i: (0, 0)),
+                pl.BlockSpec((units * UNIT, tile), lambda i: (0, i)),
+                pl.BlockSpec((units * UNIT, 2 * hidden), lambda i: (0, 0)),
             ],
             out_specs=(pl.BlockSpec((tile, hidden), lambda i: (i, 0)),) * 2,
             compiler_params=pltpu.CompilerParams(vmem_limit_bytes=60 * 2**20),

time: 87.2 us -> 84.3 us (0.967)
  Pallas kernels: 81.7 us -> 78.9 us
    pallas_call x1, Pallas kernels: 9.7 us -> 7.8 us  [fitting(): pl.pallas_call(back_kernel, out_shape=(jax.ShapeDtypeStruct((width, hidde...]
where the time goes in v4:
time: 84.3 us; the launch traced here: 84 us
  Pallas kernels  78.9 us (94%)
  local copies, waits for them, and re-layouts  2.47 us (3%)
  between operations  1.3 us (2%)
  other arithmetic  1.28 us (2%)
    pallas_call x1, Pallas kernels, moved(): pl.pallas_call(functools.partial(move_kernel, z_count), out_shape=(jax.Sh...  71.1 us
    pallas_call x1, Pallas kernels, fitting(): pl.pallas_call(back_kernel, out_shape=(jax.ShapeDtypeStruct((width, hidde...  7.8 us

profile of v4, /device:TPU:0, one launch (start us, length us, event | category | flops | bytes accessed | tf_op | source)
XLA Modules:
  0.0 84.0 jit_solution(12507508269738986049)
XLA Ops:
  0.6 1.3 %convert_bitcast_fusion.rw_hbm = f32[8,128]{1,0:T(8,128)} fusion(bf16[128,8]{0,1:T(8,128)(2,1)} %param.12), kind=kLoop, calls=%fused_computation.46 | loop fusion | flops 1024 | bytes 6144 | tf_op jit(solution)/shard_map/convert_element_type | solution.py:423
  1.9 0.0 copy-start.1
  1.9 0.0 copy-start.2
  1.9 0.0 copy-start.3
  1.9 71.1 %shard_map.94 = (bf16[192,7168]{1,0:T(8,128)(2,1)}, bf16[192,512]{1,0:T(8,128)(2,1)S(1)}, f32[8,128]{1,0:T(8,128)}, f32[8,128]{1,0:T(8,128)}) custom-call(s32[8,128]{1,0:T(8,128)} %bitcast.64, f32[8,128]{1,0:T(8,128)} %convert_bitcast_fusion.rw_hbm, bf16[128,7168]{1,0:T(8,128)(2,1)} %tok_hbm.1, bf16[128,7168]{1,0:T(8,128)(2,1)} %cot_hbm.1, ...), custom_call_target="tpu_custom_call" | custom-call | flops 4227858432 | bytes 14680064 | tf_op jit(solution)/shard_map/pallas_call | solution.py:381
  73.0 1.2 %slice.3 = f32[1,1]{1,0:T(1,128)} slice(f32[8,128]{1,0:T(8,128)} %get-tuple-element.39), slice={[0:1], [0:1]} | slice | bytes 8 | tf_op jit(solution)/shard_map/slice | solution.py:442
  74.9 0.7 copy.35
  75.6 0.0 copy-done.1
  75.6 0.0 copy-done.2
  75.6 0.0 copy-done.3
  75.6 7.8 %conditional.1 = (f32[128,8]{0,1:T(8,128)S(1)}, bf16[7168,256]{1,0:T(8,128)(2,1)}, bf16[7168,256]{1,0:T(8,128)(2,1)}) conditional(s32[]{:T(128)} %bitcast.20, (bf16[192,7168]{1,0:T(8,128)(2,1)}, bf16[192,512]{1,0:T(8,128)(2,1)S(1)}, f32[8,128]{1,0:T(8,128)S(1)}) %tuple.31, (s32[128,8]{0,1:T(8,128)S(1)}, bf16[128,7168]{1,0:T(8,128)(2,1)S(1)}, ...), branch_computations={%region_0.0_spmd, %region_1.9_spmd} | conditional | flops 2471422976 | bytes 63769240 | solution.py:442
  75.6 7.8 %branch_0_fun.1 = (bf16[7168,256]{1,0:T(8,128)(2,1)}, bf16[7168,256]{1,0:T(8,128)(2,1)}) custom-call(bf16[192,7168]{1,0:T(8,128)(2,1)} %get-tuple-element.20.rows_ref, bf16[192,512]{1,0:T(8,128)(2,1)S(1)} %get-tuple-element.21.dcat_ref), custom_call_target="tpu_custom_call" | custom-call | tf_op jit(solution)/shard_map/cond/branch_0_fun/pallas_call | solution.py:429
  83.4 0.0 copy-start.4
  83.4 0.6 copy-done.4
Async XLA Ops:
  1.9 73.7 %copy-start.1 = (bf16[128,7168]{1,0:T(8,128)(2,1)S(1)}, bf16[128,7168]{1,0:T(8,128)(2,1)}, u32[]{:S(2)}) copy-start(bf16[128,7168]{1,0:T(8,128)(2,1)} %tok_hbm.1) | copy-start | bytes 5505028
  1.9 73.7 %copy-start.2 = (s32[128,8]{0,1:T(8,128)S(1)}, s32[128,8]{0,1:T(8,128)}, u32[]{:S(2)}) copy-start(s32[128,8]{0,1:T(8,128)} %param.11) | copy-start | bytes 12292
  1.9 73.7 %copy-start.3 = (bf16[128,8]{0,1:T(8,128)(2,1)S(1)}, bf16[128,8]{0,1:T(8,128)(2,1)}, u32[]{:S(2)}) copy-start(bf16[128,8]{0,1:T(8,128)(2,1)} %param.12) | copy-start | bytes 6148
  83.4 0.6 copy-start.4

commit v5 on v4

--- a/solution.py
+++ b/solution.py
@@ -69,9 +69,9 @@
 
 
 def move_kernel(
-    z_count, ids_hbm, rw_hbm, tok_hbm, cot_hbm, wg_hbm, wu_hbm, wd_hbm,
+    z_count, ids_hbm, rw_ref, tok_hbm, cot_hbm, wg_hbm, wu_hbm, wd_hbm,
     kept_ref, dcat_ref, grad_ref, flag_ref,
-    rows_ref, ids_ref, rw_ref, tok_ref, cot_ref, wg_ref, wu_ref, wd_ref, send_ref, got_ref, pbuf, rbuf,
+    rows_ref, ids_ref, tok_ref, cot_ref, wg_ref, wu_ref, wd_ref, send_ref, got_ref, pbuf, rbuf,
     load_sem, y_send, y_recv, up_sem, down_sem, core_sem, recv_sem, back_sem, home_sem,
 ):
     y_count = 2
@@ -91,12 +91,12 @@
         pltpu.make_async_copy(src, dst, load_sem.at[i])
         for i, (src, dst) in enumerate(
             (
-                (ids_hbm, ids_ref), (rw_hbm, rw_ref), (tok_hbm, tok_ref), (cot_hbm, cot_ref),
+                (ids_hbm, ids_ref), (tok_hbm, tok_ref), (cot_hbm, cot_ref),
                 (wg_hbm, wg_ref), (wu_hbm, wu_ref), (wd_hbm, wd_ref),
             )
         )
     ]
-    for load in loads:
+    for load in loads[:3]:
         load.start()
 
     barrier = pltpu.get_barrier_semaphore()
@@ -108,7 +108,6 @@
         )
 
     loads[0].wait()
-    loads[1].wait()
     ids = ids_ref[...]
     rw = rw_ref[...].astype(jnp.float32)
     padded = -(-experts // 16) * 16
@@ -176,8 +175,10 @@
         )
 
     own = pl.ds(unit(z, c), both)
+    loads[1].wait()
     loads[2].wait()
-    loads[3].wait()
+    for load in loads[3:]:
+        load.start()
     for p in range(PIECES):
         at = pl.ds(p * piece, piece)
         x = jnp.dot(select, tok_ref[:, at], preferred_element_type=jnp.float32)
@@ -287,7 +288,7 @@
         def _():
             finish(z + hop)
 
-    for load in loads[4:]:
+    for load in loads[3:]:
         load.wait()
     for hop in range(1, z_count):
         for p in range(PIECES):
@@ -386,12 +387,11 @@
             jax.ShapeDtypeStruct(route_ids.shape[::-1], jnp.float32),
             jax.ShapeDtypeStruct((8, 128), jnp.float32),
         ),
-        in_specs=[pl.BlockSpec(memory_space=pl.ANY)] * 7,
+        in_specs=[pl.BlockSpec(memory_space=pltpu.VMEM if i == 1 else pl.ANY) for i in range(7)],
         out_specs=[pl.BlockSpec(memory_space=pltpu.VMEM)] * 4,
         scratch_shapes=[
             pltpu.VMEM((units * both, width + 128), jnp.bfloat16),
             pltpu.VMEM(route_ids.shape[::-1], jnp.int32),
-            pltpu.VMEM(route_ids.shape[::-1], jnp.float32),
             pltpu.VMEM((tok_count, width), jnp.bfloat16),
             pltpu.VMEM((tok_count, width), jnp.bfloat16),
             pltpu.VMEM((width, hidden), jnp.bfloat16),
@@ -401,7 +401,7 @@
             pltpu.VMEM((both, width + 128), jnp.bfloat16),
             pltpu.VMEM((units * message, 128), jnp.float32),
             pltpu.VMEM((group * message, 128), jnp.float32),
-            dma((7,)),
+            dma((6,)),
             dma((PIECES,)),
             dma((PIECES,)),
             dma((z_count, PIECES)),
@@ -420,7 +420,7 @@
             transcendentals=units * UNIT * hidden,
         ),
     )(
-        route_ids.T, route_weight.T.astype(jnp.float32), tokens, cotangent,
+        route_ids.T, route_weight.T, tokens, cotangent,
         gate_weight[0], up_weight[0], down_weight[0],
     )
 

time: 84.3 us -> 83.8 us (level)
  other arithmetic: 1.28 us -> 0 us
    convert_element_type x1 -> x0, other arithmetic: 1.28 us -> none  [moved(): route_weight.T.astype(jnp.float32)]
where the time goes in v5:
time: 83.8 us; the launch traced here: 83.4 us
  Pallas kernels  79.6 us (95%)
  local copies, waits for them, and re-layouts  2.47 us (3%)
  between operations  1.32 us (2%)
    pallas_call x1, Pallas kernels, moved(): pl.pallas_call(functools.partial(move_kernel, z_count), out_shape=(jax.Sh...  71.8 us
    pallas_call x1, Pallas kernels, fitting(): pl.pallas_call(back_kernel, out_shape=(jax.ShapeDtypeStruct((width, hidde...  7.81 us

profile of v5, /device:TPU:0, one launch (start us, length us, event | category | flops | bytes accessed | tf_op | source)
XLA Modules:
  0.0 83.4 jit_solution(8134745063019962355)
XLA Ops:
  0.6 0.0 copy-start.1
  0.6 0.0 copy-start.2
  0.7 0.0 copy-start.4
  0.7 71.8 %shard_map.94 = (bf16[192,7168]{1,0:T(8,128)(2,1)}, bf16[192,512]{1,0:T(8,128)(2,1)S(1)}, f32[8,128]{1,0:T(8,128)}, f32[8,128]{1,0:T(8,128)}) custom-call(s32[8,128]{1,0:T(8,128)} %bitcast.63, bf16[8,128]{1,0:T(8,128)(2,1)} %bitcast.65, bf16[128,7168]{1,0:T(8,128)(2,1)} %tok_hbm.1, bf16[128,7168]{1,0:T(8,128)(2,1)} %cot_hbm.1, bf16[7168,256]{1,0:T(8,128)(2,1)} %bitcast.58, ...), custom_call_target="tpu_custom_call" | custom-call | flops 4227858432 | bytes 14680064 | tf_op jit(solution)/shard_map/pallas_call | solution.py:382
  72.5 1.2 %slice.3 = f32[1,1]{1,0:T(1,128)} slice(f32[8,128]{1,0:T(8,128)} %get-tuple-element.39), slice={[0:1], [0:1]} | slice | bytes 8 | tf_op jit(solution)/shard_map/slice | solution.py:442
  74.3 0.7 copy.35
  75.0 0.0 copy-done.1
  75.0 0.0 copy-done.2
  75.0 0.0 copy-done.4
  75.0 7.8 %conditional.1 = (f32[128,8]{0,1:T(8,128)S(1)}, bf16[7168,256]{1,0:T(8,128)(2,1)}, bf16[7168,256]{1,0:T(8,128)(2,1)}) conditional(s32[]{:T(128)} %bitcast.20, (bf16[192,7168]{1,0:T(8,128)(2,1)}, bf16[192,512]{1,0:T(8,128)(2,1)S(1)}, f32[8,128]{1,0:T(8,128)S(1)}) %tuple.31, (s32[128,8]{0,1:T(8,128)S(1)}, bf16[128,7168]{1,0:T(8,128)(2,1)S(1)}, ...), branch_computations={%region_0.0_spmd, %region_1.9_spmd} | conditional | flops 2471422976 | bytes 63769240 | solution.py:442
  75.0 7.8 %branch_0_fun.1 = (bf16[7168,256]{1,0:T(8,128)(2,1)}, bf16[7168,256]{1,0:T(8,128)(2,1)}) custom-call(bf16[192,7168]{1,0:T(8,128)(2,1)} %get-tuple-element.20.rows_ref, bf16[192,512]{1,0:T(8,128)(2,1)S(1)} %get-tuple-element.21.dcat_ref), custom_call_target="tpu_custom_call" | custom-call | tf_op jit(solution)/shard_map/cond/branch_0_fun/pallas_call | solution.py:429
  82.8 0.0 copy-start.3
  82.8 0.6 copy-done.3
Async XLA Ops:
  0.6 74.4 %copy-start.1 = (bf16[128,7168]{1,0:T(8,128)(2,1)S(1)}, bf16[128,7168]{1,0:T(8,128)(2,1)}, u32[]{:S(2)}) copy-start(bf16[128,7168]{1,0:T(8,128)(2,1)} %tok_hbm.1) | copy-start | bytes 5505028
  0.6 74.4 %copy-start.2 = (s32[128,8]{0,1:T(8,128)S(1)}, s32[128,8]{0,1:T(8,128)}, u32[]{:S(2)}) copy-start(s32[128,8]{0,1:T(8,128)} %param.11) | copy-start | bytes 12292
  0.7 74.4 %copy-start.4 = (bf16[128,8]{0,1:T(8,128)(2,1)S(1)}, bf16[128,8]{0,1:T(8,128)(2,1)}, u32[]{:S(2)}) copy-start(bf16[128,8]{0,1:T(8,128)(2,1)} %param.12) | copy-start | bytes 6148
  82.8 0.6 copy-start.3
